TPU v7x, 1024 devices: a whole 4x8x16 slice. The times are simulated.
1024 devices in a mesh: rx: 4 (over x_hi, core), space: 256 (over x_lo, y, z).
Axes of the slice: x: 4 (x_hi: 2, x_lo: 2; x = x_hi * 2 + x_lo), y: 8, z: 16, core: 2. Of those that a mesh axis runs over, the one named last changes fastest.
Arguments:
- conductivity: float32 [768, 32, 128], P('space'), may hold values from 0.1 to 1
- background: float32 [4, 2, 3, 768, 32, 128], P(None, None, None, 'space'), may hold values from -6 to 6
- warm_start: float32 [8, 2, 3, 768, 32, 128], P('rx', None, None, 'space'), may hold values from -8 to 8
- data_weight: float32 [8, 2, 3], P('rx'), may hold values from -2560 to 2560
- recv_cell: int32 [8], P('rx'), may hold values from 0 to 3145727
- src_group: int32 [8], P('rx'), may hold values from 0 to 3
- group_freq: int32 [4], replicated, may hold values from 0 to 7
Outputs:
- block: float32 [16, 16], P('rx')
- smoothed: bfloat16 [8, 2, 768, 32, 128], P('rx', None, 'space')
All inputs are finite; a program needn't handle non-finite values.
Results may differ from a plain program's by a relative error of at most 0.01.
Values may be sent and summed in bfloat16 or wider, within the bound.
A program may use at most 32 MiB of HBM per device.

v0:
```python
import jax
import jax.numpy as jnp
from jax import lax
from jax.sharding import PartitionSpec as P

ITERS = 3


RELAX = 0.2
KAPPA = 0.1


def with_halo(x, sides, width):
    for axis, dim in sides:
        peers, length = (lax.axis_size(axis), x.shape[dim])
        up = [(i, (i + 1) % peers) for i in range(peers - 1)]
        down = [(j, i) for i, j in up]
        last = lax.slice_in_dim(x, length - width, length, axis=dim)
        leading = lax.slice_in_dim(x, 0, width, axis=dim)
        before = lax.ppermute(last, axis, up)
        after = lax.ppermute(leading, axis, down)
        x = jnp.concatenate([before, x, after], axis=dim)
    return x


def forward_y(f):
    return jnp.concatenate([f[..., 1:, :] - f[..., :-1, :], -f[..., -1:, :]], axis=-2)


def forward_z(f):
    return jnp.concatenate([f[..., 1:] - f[..., :-1], -f[..., -1:]], axis=-1)


def backward_y(f):
    return jnp.concatenate([f[..., :1, :], f[..., 1:, :] - f[..., :-1, :]], axis=-2)


def backward_z(f):
    return jnp.concatenate([f[..., :1], f[..., 1:] - f[..., :-1]], axis=-1)


def curl_curl(padded):
    comp_x = padded[..., 0, :, :, :]
    comp_y = padded[..., 1, :, :, :]
    comp_z = padded[..., 2, :, :, :]
    low_x = comp_x[..., :-1, :, :]
    low_y = comp_y[..., :-1, :, :]
    low_z = comp_z[..., :-1, :, :]
    mag_x = forward_y(low_z) - forward_z(low_y)
    mag_y = forward_z(low_x) - (comp_z[..., 1:, :, :] - comp_z[..., :-1, :, :])
    mag_z = comp_y[..., 1:, :, :] - comp_y[..., :-1, :, :] - forward_y(low_x)
    curl_x = backward_y(mag_z[..., 1:, :, :]) - backward_z(mag_y[..., 1:, :, :])
    curl_y = backward_z(mag_x[..., 1:, :, :]) - (mag_z[..., 1:, :, :] - mag_z[..., :-1, :, :])
    curl_z = mag_y[..., 1:, :, :] - mag_y[..., :-1, :, :] - backward_y(mag_x[..., 1:, :, :])
    return jnp.stack([curl_x, curl_y, curl_z], axis=-4)


def operate(adjoint, padded, coef):
    curl = curl_curl(padded)
    real_part = curl[..., 0, :, :, :, :] - coef * adjoint[..., 1, :, :, :, :]
    imag_part = curl[..., 1, :, :, :, :] + coef * adjoint[..., 0, :, :, :, :]
    return jnp.stack([real_part, imag_part], axis=-5)


def sensitivity(adjoint, field, coef):
    field_re = field[..., 0, :, :, :, :]
    field_im = field[..., 1, :, :, :, :]
    adj_re = adjoint[..., 0, :, :, :, :]
    adj_im = adjoint[..., 1, :, :, :, :]
    prod_re = jnp.sum(field_re * adj_re - field_im * adj_im, axis=-4)
    prod_im = jnp.sum(field_re * adj_im + field_im * adj_re, axis=-4)
    return (coef * jnp.stack([prod_re, prod_im], axis=-4)).astype(jnp.bfloat16)


def neighbours_y(f):
    zeros = jnp.zeros_like(f[..., :1, :])
    return jnp.concatenate([f[..., 1:, :], zeros], axis=-2) + jnp.concatenate(
        [zeros, f[..., :-1, :]], axis=-2
    )


def neighbours_z(f):
    zeros = jnp.zeros_like(f[..., :1])
    return jnp.concatenate([f[..., 1:], zeros], axis=-1) + jnp.concatenate(
        [zeros, f[..., :-1]], axis=-1
    )


def smooth_step(padded):
    centre = padded[..., 1:-1, :, :]
    near = (
        padded[..., 2:, :, :] + padded[..., :-2, :, :] + neighbours_y(centre) + neighbours_z(centre)
    )
    return centre + KAPPA * (near - 6.0 * centre)


def point_terms(data_weight, recv_cell, first_plane, planes, height, breadth):
    plane_ids = first_plane + jnp.arange(planes, dtype=jnp.int32)
    inner = jnp.arange(height * breadth, dtype=jnp.int32).reshape(height, breadth)
    flat = plane_ids[:, None, None] * (height * breadth) + inner[None]
    point = (flat[None] == recv_cell[:, None, None, None]).astype(jnp.float32)
    return data_weight[:, :, :, None, None, None] * point[:, None, None]


def shards(conductivity, background, warm_start, data_weight, recv_cell, src_group, group_freq):
    count = warm_start.shape[0]
    groups = background.shape[0]
    depth, height, breadth = conductivity.shape
    cells = depth * height * breadth
    selector = (src_group[:, None] == jnp.arange(groups, dtype=jnp.int32)[None, :]).astype(
        jnp.float32
    )
    freq_value = jnp.sum(selector * group_freq.astype(jnp.float32)[None, :], axis=1)
    angular = 0.25 * jnp.power(jnp.float32(1.25), freq_value)
    coef = angular[:, None, None, None, None] * conductivity[None, None]
    field = jnp.sum(selector[:, :, None, None, None, None, None] * background[None], axis=1)
    adjoint = warm_start
    source_term = point_terms(
        data_weight, recv_cell, lax.axis_index("space") * depth, depth, height, breadth
    )
    for sweep in range(ITERS):
        padded = with_halo(adjoint, (("space", 3),), 1)
        adjoint = adjoint + RELAX * (source_term - operate(adjoint, padded, coef))
    rows = sensitivity(adjoint, field, coef)
    value = rows.astype(jnp.float32)
    for sweep in range(2):
        value = smooth_step(with_halo(value, (("space", 2),), 1))
    smoothed = value.astype(jnp.bfloat16)
    flat_rows = rows.reshape(2 * count, cells)
    flat_smooth = smoothed.reshape(2 * count, cells)
    partial_block = jnp.einsum(
        "rc,kc->rk",
        flat_rows,
        lax.all_gather(flat_smooth, "rx", axis=0, tiled=True),
        preferred_element_type=jnp.float32,
    )
    total = lax.psum(partial_block, "space")
    block = total / (cells * lax.axis_size("space"))
    return (block, smoothed)


def solution(mesh):
    in_specs = (
        P("space", None, None),
        P(None, None, None, "space", None, None),
        P("rx", None, None, "space", None, None),
        P("rx", None, None),
        P("rx"),
        P("rx"),
        P(),
    )
    out_specs = (P("rx", None), P("rx", None, "space", None, None))
    return jax.shard_map(shards, mesh=mesh, in_specs=in_specs, out_specs=out_specs, check_vma=False)
```

profile of v0, /device:TPU:6, one launch (start us, length us, event | category | flops | bytes accessed | tf_op | source)
XLA Modules:
  0.0 721.3 jit_solution(12191641280395338768)
XLA Ops:
  0.7 1.1 fusion.56
  1.8 4.3 collective-permute-start
  6.1 19.0 %collective-permute-start.1 = (f32[2,2,3,1,32,128]{5,4,3,1,0,2:T(8,128)S(1)}, f32[2,2,3,1,32,128]{5,4,3,1,0,2:T(8,128)S(1)}, u32[]{:S(2)}, u32[]{:S(2)}) collective-permute-start(f32[2,2,3,1,32,128]{5,4,3,1,0,2:T(8,128)S(1)} %copy.94), channel_id=1, source_target_pairs={{1,0},{2,1},{3,2},{4,3},{5,4},{6,5},{7,6},{8,7},{9,8},{10,9},{11,1... | collective-permute-start | bytes 589832 | tf_op jit(solution)/shard_map/ppermute | solution.py:21
  25.7 2.4 collective-permute-done
  28.2 1.1 collective-permute-done.1
  32.3 1.9 collective-permute-start.2
  34.2 8.6 %collective-permute-start.3 = (f32[2,2,3,1,32,128]{5,4,3,1,0,2:T(8,128)S(1)}, f32[2,2,3,1,32,128]{5,4,3,1,0,2:T(8,128)S(1)}, u32[]{:S(2)}, u32[]{:S(2)}) collective-permute-start(f32[2,2,3,1,32,128]{5,4,3,1,0,2:T(8,128)S(1)} %copy.96), channel_id=1, source_target_pairs={{1,0},{2,1},{3,2},{4,3},{5,4},{6,5},{7,6},{8,7},{9,8},{10,9},{11,1... | collective-permute-start | bytes 589832 | tf_op jit(solution)/shard_map/ppermute | solution.py:21
  42.8 2.1 collective-permute-done.2
  45.1 1.0 collective-permute-done.3
  47.2 0.8 slice_subtract_fusion.28
  48.0 0.7 slice.735
  48.9 0.8 fusion.39
  50.1 1.0 fusion.38
  51.2 1.0 fusion.48
  52.7 2.1 collective-permute-start.4
  54.9 1.1 multiply_reduce_fusion
  56.0 8.6 %collective-permute-start.5 = (f32[2,2,3,1,32,128]{5,4,3,1,0,2:T(8,128)S(1)}, f32[2,2,3,1,32,128]{5,4,3,1,0,2:T(8,128)S(1)}, u32[]{:S(2)}, u32[]{:S(2)}) collective-permute-start(f32[2,2,3,1,32,128]{5,4,3,1,0,2:T(8,128)S(1)} %copy.98), channel_id=1, source_target_pairs={{1,0},{2,1},{3,2},{4,3},{5,4},{6,5},{7,6},{8,7},{9,8},{10,9},{11,1... | collective-permute-start | bytes 589832 | tf_op jit(solution)/shard_map/ppermute | solution.py:21
  65.4 2.4 collective-permute-done.5
  68.8 0.8 slice_subtract_fusion.22
  69.7 0.7 slice.775
  70.4 0.7 fusion.34
  71.3 0.8 fusion.33
  72.5 1.2 fusion.32
  74.4 0.7 copy-done.1
  75.4 1.9 collective-permute-start.7
  77.3 8.6 %collective-permute-start.6 = (f32[2,2,1,32,128]{4,3,2,1,0:T(8,128)S(1)}, f32[2,2,1,32,128]{4,3,2,1,0:T(8,128)S(1)}, u32[]{:S(2)}, u32[]{:S(2)}) collective-permute-start(f32[2,2,1,32,128]{4,3,2,1,0:T(8,128)S(1)} %get-tuple-element.37), channel_id=1, source_target_pairs={{1,0},{2,1},{3,2},{4,3},{5,4},{6,5},{7,6},{8,7},{9,8},{10,9},{11,1... | collective-permute-start | bytes 196616 | tf_op jit(solution)/shard_map/ppermute | solution.py:21
  86.3 1.6 collective-permute-done.6
  88.1 1.9 collective-permute-start.9
  90.0 8.5 %collective-permute-start.8 = (f32[2,2,1,32,128]{4,3,2,1,0:T(8,128)S(1)}, f32[2,2,1,32,128]{4,3,2,1,0:T(8,128)S(1)}, u32[]{:S(2)}, u32[]{:S(2)}) collective-permute-start(f32[2,2,1,32,128]{4,3,2,1,0:T(8,128)S(1)} %get-tuple-element.31), channel_id=1, source_target_pairs={{1,0},{2,1},{3,2},{4,3},{5,4},{6,5},{7,6},{8,7},{9,8},{10,9},{11,1... | collective-permute-start | bytes 196616 | tf_op jit(solution)/shard_map/ppermute | solution.py:21
  98.8 1.6 collective-permute-done.8
  100.6 7.7 %all-gather = bf16[4,4,12288]{2,1,0:T(4,128)(2,1)S(1)} all-gather(bf16[1,4,12288]{2,1,0:T(4,128)(2,1)S(1)} %reshape.239), channel_id=1, replica_groups=mesh['rx'=4,'space'=256] {'rx'}, dimensions={0}, use_global_device_ids=true | all-gather | bytes 491520 | tf_op jit(solution)/shard_map/all_gather | solution.py:134
  108.6 612.1 %psum.7 = f32[4,16]{1,0:T(4,128)S(1)} all-reduce(f32[4,16]{1,0:T(4,128)S(1)} %fusion.63), channel_id=1, replica_groups=mesh['rx'=4,'space'=256] {'space'}, use_global_device_ids=true, to_apply=%region_4.0 | all-reduce | flops 64 | bytes 512 | tf_op jit(solution)/shard_map/psum | solution.py:137
  (137 shorter events, 10.9 us)
Async XLA Ops:
  0.6 27.5 %copy-start = (f32[2,2,3,3,32,128]{5,4,3,2,1,0:T(8,128)S(1)}, f32[2,2,3,3,32,128]{5,4,3,2,1,0:T(8,128)}, u32[]{:S(2)}) copy-start(f32[2,2,3,3,32,128]{5,4,3,2,1,0:T(8,128)} %param.9) | copy-start | bytes 1769476
  0.6 24.5 %copy-start.10 = (s32[4]{0:T(128)S(1)}, s32[4]{0:T(128)}, u32[]{:S(2)}) copy-start(s32[4]{0:T(128)} %param.13) | copy-start | bytes 52
  0.7 24.6 %copy-start.11 = (s32[2]{0:T(128)S(1)}, s32[2]{0:T(128)}, u32[]{:S(2)}) copy-start(s32[2]{0:T(128)} %param.12) | copy-start | bytes 28
  0.7 24.8 %copy-start.8 = (f32[3,32,128]{2,1,0:T(8,128)S(1)}, f32[3,32,128]{2,1,0:T(8,128)}, u32[]{:S(2)}) copy-start(f32[3,32,128]{2,1,0:T(8,128)} %param.7) | copy-start | bytes 147460
  0.7 24.9 %copy-start.9 = (s32[2]{0:T(128)S(1)}, s32[2]{0:T(128)}, u32[]{:S(2)}) copy-start(s32[2]{0:T(128)} %param.11) | copy-start | bytes 28
  1.8 26.3 %collective-permute-start = (f32[2,2,3,1,32,128]{5,4,3,1,0,2:T(8,128)S(1)}, f32[2,2,3,1,32,128]{5,4,3,1,0,2:T(8,128)S(1)}, u32[]{:S(2)}, u32[]{:S(2)}) collective-permute-start(f32[2,2,3,1,32,128]{5,4,3,1,0,2:T(8,128)S(1)} %copy.93), channel_id=1, source_target_pairs={{0,1},{1,2},{2,3},{3,4},{4,5},{5,6},{6,7},{7,8},{8,9},{9,10},{10,1... | collective-permute-start | bytes 589832 | tf_op jit(solution)/shard_map/ppermute | solution.py:20
  6.1 23.2 %collective-permute-start.1 = (f32[2,2,3,1,32,128]{5,4,3,1,0,2:T(8,128)S(1)}, f32[2,2,3,1,32,128]{5,4,3,1,0,2:T(8,128)S(1)}, u32[]{:S(2)}, u32[]{:S(2)}) collective-permute-start(f32[2,2,3,1,32,128]{5,4,3,1,0,2:T(8,128)S(1)} %copy.94), channel_id=1, source_target_pairs={{1,0},{2,1},{3,2},{4,3},{5,4},{6,5},{7,6},{8,7},{9,8},{10,9},{11,1... | collective-permute-start | bytes 589832 | tf_op jit(solution)/shard_map/ppermute | solution.py:21
  31.4 0.7 copy-start.7
  32.3 12.6 %collective-permute-start.2 = (f32[2,2,3,1,32,128]{5,4,3,1,0,2:T(8,128)S(1)}, f32[2,2,3,1,32,128]{5,4,3,1,0,2:T(8,128)S(1)}, u32[]{:S(2)}, u32[]{:S(2)}) collective-permute-start(f32[2,2,3,1,32,128]{5,4,3,1,0,2:T(8,128)S(1)} %copy.95), channel_id=1, source_target_pairs={{0,1},{1,2},{2,3},{3,4},{4,5},{5,6},{6,7},{7,8},{8,9},{9,10},{10,1... | collective-permute-start | bytes 589832 | tf_op jit(solution)/shard_map/ppermute | solution.py:20
  34.2 11.9 %collective-permute-start.3 = (f32[2,2,3,1,32,128]{5,4,3,1,0,2:T(8,128)S(1)}, f32[2,2,3,1,32,128]{5,4,3,1,0,2:T(8,128)S(1)}, u32[]{:S(2)}, u32[]{:S(2)}) collective-permute-start(f32[2,2,3,1,32,128]{5,4,3,1,0,2:T(8,128)S(1)} %copy.96), channel_id=1, source_target_pairs={{1,0},{2,1},{3,2},{4,3},{5,4},{6,5},{7,6},{8,7},{9,8},{10,9},{11,1... | collective-permute-start | bytes 589832 | tf_op jit(solution)/shard_map/ppermute | solution.py:21
  48.9 1.2 copy-start.5
  52.7 2.2 copy-start.2
  52.7 12.4 %collective-permute-start.4 = (f32[2,2,3,1,32,128]{5,4,3,1,0,2:T(8,128)S(1)}, f32[2,2,3,1,32,128]{5,4,3,1,0,2:T(8,128)S(1)}, u32[]{:S(2)}, u32[]{:S(2)}) collective-permute-start(f32[2,2,3,1,32,128]{5,4,3,1,0,2:T(8,128)S(1)} %copy.97), channel_id=1, source_target_pairs={{0,1},{1,2},{2,3},{3,4},{4,5},{5,6},{6,7},{7,8},{8,9},{9,10},{10,1... | collective-permute-start | bytes 589832 | tf_op jit(solution)/shard_map/ppermute | solution.py:20
  56.0 11.8 %collective-permute-start.5 = (f32[2,2,3,1,32,128]{5,4,3,1,0,2:T(8,128)S(1)}, f32[2,2,3,1,32,128]{5,4,3,1,0,2:T(8,128)S(1)}, u32[]{:S(2)}, u32[]{:S(2)}) collective-permute-start(f32[2,2,3,1,32,128]{5,4,3,1,0,2:T(8,128)S(1)} %copy.98), channel_id=1, source_target_pairs={{1,0},{2,1},{3,2},{4,3},{5,4},{6,5},{7,6},{8,7},{9,8},{10,9},{11,1... | collective-permute-start | bytes 589832 | tf_op jit(solution)/shard_map/ppermute | solution.py:21
  72.4 1.3 copy-start.3
  72.4 1.3 copy-start.4
  74.0 1.1 copy-start.1
  75.4 10.9 %collective-permute-start.7 = (f32[2,2,1,32,128]{4,3,2,1,0:T(8,128)S(1)}, f32[2,2,1,32,128]{4,3,2,1,0:T(8,128)S(1)}, u32[]{:S(2)}, u32[]{:S(2)}) collective-permute-start(f32[2,2,1,32,128]{4,3,2,1,0:T(8,128)S(1)} %get-tuple-element.38), channel_id=1, source_target_pairs={{0,1},{1,2},{2,3},{3,4},{4,5},{5,6},{6,7},{7,8},{8,9},{9,10},{10,1... | collective-permute-start | bytes 196616 | tf_op jit(solution)/shard_map/ppermute | solution.py:20
  77.3 10.5 %collective-permute-start.6 = (f32[2,2,1,32,128]{4,3,2,1,0:T(8,128)S(1)}, f32[2,2,1,32,128]{4,3,2,1,0:T(8,128)S(1)}, u32[]{:S(2)}, u32[]{:S(2)}) collective-permute-start(f32[2,2,1,32,128]{4,3,2,1,0:T(8,128)S(1)} %get-tuple-element.37), channel_id=1, source_target_pairs={{1,0},{2,1},{3,2},{4,3},{5,4},{6,5},{7,6},{8,7},{9,8},{10,9},{11,1... | collective-permute-start | bytes 196616 | tf_op jit(solution)/shard_map/ppermute | solution.py:21
  88.1 10.7 %collective-permute-start.9 = (f32[2,2,1,32,128]{4,3,2,1,0:T(8,128)S(1)}, f32[2,2,1,32,128]{4,3,2,1,0:T(8,128)S(1)}, u32[]{:S(2)}, u32[]{:S(2)}) collective-permute-start(f32[2,2,1,32,128]{4,3,2,1,0:T(8,128)S(1)} %get-tuple-element.32), channel_id=1, source_target_pairs={{0,1},{1,2},{2,3},{3,4},{4,5},{5,6},{6,7},{7,8},{8,9},{9,10},{10,1... | collective-permute-start | bytes 196616 | tf_op jit(solution)/shard_map/ppermute | solution.py:20
  90.0 10.4 %collective-permute-start.8 = (f32[2,2,1,32,128]{4,3,2,1,0:T(8,128)S(1)}, f32[2,2,1,32,128]{4,3,2,1,0:T(8,128)S(1)}, u32[]{:S(2)}, u32[]{:S(2)}) collective-permute-start(f32[2,2,1,32,128]{4,3,2,1,0:T(8,128)S(1)} %get-tuple-element.31), channel_id=1, source_target_pairs={{1,0},{2,1},{3,2},{4,3},{5,4},{6,5},{7,6},{8,7},{9,8},{10,9},{11,1... | collective-permute-start | bytes 196616 | tf_op jit(solution)/shard_map/ppermute | solution.py:21
  100.6 620.7 %copy-start.6 = (bf16[2,2,3,32,128]{4,3,2,1,0:T(8,128)(2,1)}, bf16[2,2,3,32,128]{4,3,2,1,0:T(8,128)(2,1)S(1)}, u32[]{:S(2)}) copy-start(bf16[2,2,3,32,128]{4,3,2,1,0:T(8,128)(2,1)S(1)} %fusion.22) | copy-start | bytes 294916
where the time goes:
time: 722 us; the launch traced here: 721 us
  blocking collectives  620 us (86%)
  starting transfers between devices  65.4 us (9%)
  other arithmetic  15.5 us (2%)
  waiting for transfers between devices  13.2 us (2%)
    psum x1, blocking collectives, shards(): total = lax.psum(partial_block, 'space')  612 us
    ppermute x5, starting transfers between devices, with_halo(): after = lax.ppermute(leading, axis, down)  53.3 us
  transfers between devices with their start and end apart: 10, of which 10 were waited for; matrix products, arithmetic and copies ran while one was open for 0% of the time, Pallas kernels for 0%

commit v1 on v0

v1 whole, which is shorter than its diff:
```python
import functools

import jax
import jax.numpy as jnp
from jax import lax
from jax.experimental import pallas as pl
from jax.experimental.pallas import tpu as pltpu
from jax.sharding import PartitionSpec as P

ITERS = 3
RELAX = 0.2
KAPPA = 0.1
MESH = pl.DeviceIdType.MESH


def kernel(
    peers,
    lines,
    rx_peers,
    cond_hbm,
    back_hbm,
    warm_hbm,
    weight_hbm,
    cell_hbm,
    group_hbm,
    freq_hbm,
    block_ref,
    smooth_hbm,
    cond,
    back,
    warm,
    weight,
    cell,
    group,
    freq,
    send,
    csend,
    land,
    cland,
    first,
    second,
    third,
    rows,
    rland,
    smooth,
    sums,
    line_sums,
    plane_sums,
    load_sem,
    out_sem,
    send_sem,
    recv_sem,
    rsend_sem,
    rrecv_sem,
    gsend_sem,
    grecv_sem,
    ssend_sem,
    srecv_sem,
):
    depth = cond.shape[0]
    height, breadth = cond.shape[1:]
    count = warm.shape[0]
    rx = lax.axis_index("rx")
    me = lax.axis_index("space")
    columns = peers // lines
    line = me // columns
    column = me % columns
    after = (rx, (me + 1) % peers)
    before = (rx, (me + peers - 1) % peers)
    others = [((rx + k) % rx_peers, me) for k in range(1, rx_peers)]
    along = [(rx, line * columns + (column + k) % columns) for k in range(1, columns)]
    across = [(rx, ((line + k) % lines) * columns + column) for k in range(1, lines)]

    loads = [
        pltpu.make_async_copy(src, dst, load_sem.at[i])
        for i, (src, dst) in enumerate(
            (
                (warm_hbm, warm),
                (cond_hbm, cond),
                (weight_hbm, weight),
                (cell_hbm, cell),
                (group_hbm, group),
                (freq_hbm, freq),
                (back_hbm, back),
            )
        )
    ]
    for load in loads:
        load.start()
    barrier = pltpu.get_barrier_semaphore()
    partners = [before, after] + others + along + across
    for partner in partners:
        pl.semaphore_signal(barrier, inc=1, device_id=partner, device_id_type=MESH)

    for load in loads[:2]:
        load.wait()
    csend[...] = cond[...].astype(jnp.bfloat16)

    def pack(s, carry):
        for p in range(2):
            for c in range(3):
                send[:, c, 2 * s + p] = warm[s, p, c].astype(jnp.bfloat16)
        return carry

    lax.fori_loop(0, count, pack, 0)
    pl.semaphore_wait(barrier, len(partners))

    copies = []
    for k in range(depth):
        for way, target in ((0, after), (1, before)):
            plane = depth - 1 - k if way == 0 else k
            copies.append(
                pltpu.make_async_remote_copy(
                    send.at[plane],
                    land.at[way, plane],
                    send_sem.at[way, k],
                    recv_sem.at[way, k],
                    device_id=target,
                    device_id_type=MESH,
                )
            )
    ccopies = [
        pltpu.make_async_remote_copy(
            csend,
            cland.at[way],
            send_sem.at[way, depth],
            recv_sem.at[way, depth],
            device_id=target,
            device_id_type=MESH,
        )
        for way, target in ((0, after), (1, before))
    ]
    for copy in copies[:2] + ccopies + copies[2:]:
        copy.start()

    for load in loads[2:]:
        load.wait()
    has_before = (me > 0).astype(jnp.float32)
    has_after = (me < peers - 1).astype(jnp.float32)
    iy = lax.broadcasted_iota(jnp.int32, (height, breadth), 0)
    iz = lax.broadcasted_iota(jnp.int32, (height, breadth), 1)
    flat = iy * breadth + iz

    def y_up(f):
        return jnp.where(iy == height - 1, 0.0, pltpu.roll(f, height - 1, 0))

    def y_down(f):
        return jnp.where(iy == 0, 0.0, pltpu.roll(f, 1, 0))

    def z_up(f):
        return jnp.where(iz == breadth - 1, 0.0, pltpu.roll(f, breadth - 1, 1))

    def z_down(f):
        return jnp.where(iz == 0, 0.0, pltpu.roll(f, 1, 1))

    def angular_of(s):
        k = freq[group[s]]
        low = jnp.where(k % 2 == 1, jnp.float32(1.25), jnp.float32(1.0))
        mid = jnp.where((k // 2) % 2 == 1, jnp.float32(1.25**2), jnp.float32(1.0))
        top = jnp.where((k // 4) % 2 == 1, jnp.float32(1.25**4), jnp.float32(1.0))
        return 0.25 * (low * mid * top)

    def guard(plane, f):
        if plane < depth:
            return f * has_before
        if plane >= 2 * depth:
            return f * has_after
        return f

    def start_plane(s, p, c, plane):
        if plane < depth:
            return guard(plane, land[0, plane, c, 2 * s + p].astype(jnp.float32))
        if plane >= 2 * depth:
            return guard(plane, land[1, plane - 2 * depth, c, 2 * s + p].astype(jnp.float32))
        return warm[s, p, c, plane - depth]

    def cond_plane(plane):
        if plane < depth:
            return cland[0, plane].astype(jnp.float32)
        if plane >= 2 * depth:
            return cland[1, plane - 2 * depth].astype(jnp.float32)
        return cond[plane - depth]

    def stored(buffer):
        return lambda s, p, c, plane: buffer[2 * s + p, c, plane]

    def sweep(source, target, low, high):
        def one(i, carry):
            s, p = i // 2, i % 2
            turn = (1 - 2 * p).astype(jnp.float32) * (RELAX * angular_of(s))
            old = {
                (c, plane): source(s, p, c, plane)
                for plane in range(low - 1, high + 1)
                for c in range(3)
            }

            def mag_y(plane):
                ex = old[0, plane]
                return (z_up(ex) - ex) - (old[2, plane + 1] - old[2, plane])

            def mag_z(plane):
                ex = old[0, plane]
                return (old[1, plane + 1] - old[1, plane]) - (y_up(ex) - ex)

            hy_low, hz_low = mag_y(low - 1), mag_z(low - 1)
            for plane in range(low, high):
                ey, ez = old[1, plane], old[2, plane]
                hx = (y_up(ez) - ez) - (z_up(ey) - ey)
                hy, hz = mag_y(plane), mag_z(plane)
                curl = (
                    (hz - y_down(hz)) - (hy - z_down(hy)),
                    (hx - z_down(hx)) - (hz - hz_low),
                    (hy - hy_low) - (hx - y_down(hx)),
                )
                hy_low, hz_low = hy, hz
                factor = turn * cond_plane(plane)
                here = cell[s] - (me * depth + plane - depth) * (height * breadth)
                point = flat == here
                for c in range(3):
                    other = source(s, 1 - p, c, plane)
                    term = jnp.where(point, RELAX * weight[s, p, c], 0.0)
                    new = old[c, plane] + term - RELAX * curl[c] + factor * other
                    target[i, c, plane] = guard(plane, new)
            return carry

        lax.fori_loop(0, 2 * count, one, 0)

    own = (depth, 2 * depth)
    for copy in copies + ccopies:
        copy.wait_recv()
    sweep(start_plane, first, own[0] - 2, own[1] + 2)
    sweep(stored(first), second, own[0] - 1, own[1] + 1)
    sweep(stored(second), third, own[0], own[1])

    def products(s, carry):
        g = group[s]
        angular = angular_of(s)
        for plane in range(depth):
            real = jnp.zeros((height, breadth), jnp.float32)
            imag = jnp.zeros((height, breadth), jnp.float32)
            for c in range(3):
                fr, fi = back[g, 0, c, plane], back[g, 1, c, plane]
                ar, ai = third[2 * s, c, depth + plane], third[2 * s + 1, c, depth + plane]
                real += fr * ar - fi * ai
                imag += fr * ai + fi * ar
            coef = angular * cond[plane]
            rows[rx, plane, 2 * s] = (coef * real).astype(jnp.bfloat16)
            rows[rx, plane, 2 * s + 1] = (coef * imag).astype(jnp.bfloat16)
        return carry

    lax.fori_loop(0, count, products, 0)

    halo = [
        pltpu.make_async_remote_copy(
            rows.at[rx, pl.ds(start, 2)],
            rland.at[way],
            rsend_sem.at[way],
            rrecv_sem.at[way],
            device_id=target,
            device_id_type=MESH,
        )
        for way, target, start in ((0, after, depth - 2), (1, before, 0))
    ]
    gather = [
        pltpu.make_async_remote_copy(
            rows.at[rx],
            rows.at[rx],
            gsend_sem.at[k],
            grecv_sem.at[k],
            device_id=target,
            device_id_type=MESH,
        )
        for k, target in enumerate(others)
    ]
    for copy in halo + gather:
        copy.start()
    for copy in halo:
        copy.wait_recv()

    def smoothing(r, carry):
        planes = (
            [rland[0, k, r].astype(jnp.float32) * has_before for k in range(2)]
            + [rows[rx, k, r].astype(jnp.float32) for k in range(depth)]
            + [rland[1, k, r].astype(jnp.float32) * has_after for k in range(2)]
        )
        for step in range(2):
            ends = [planes[0], planes[-1]]
            planes = [
                planes[k]
                + KAPPA
                * (
                    planes[k - 1]
                    + planes[k + 1]
                    + y_up(planes[k])
                    + y_down(planes[k])
                    + z_up(planes[k])
                    + z_down(planes[k])
                    - 6.0 * planes[k]
                )
                for k in range(1, len(planes) - 1)
            ]
            if step == 0:
                planes[0] = planes[0] * has_before
                planes[-1] = planes[-1] * has_after
        for k in range(depth):
            smooth[r, k] = planes[k].astype(jnp.bfloat16)
        return carry

    lax.fori_loop(0, 2 * count, smoothing, 0)
    out = pltpu.make_async_copy(smooth, smooth_hbm, out_sem)
    out.start()

    for copy in gather:
        copy.wait_recv()

    def dots(b, carry):
        peer, r = b // (2 * count), b % (2 * count)
        for a in range(2 * count):
            total = jnp.zeros((8, breadth), jnp.float32)
            for k in range(depth):
                product = smooth[a, k].astype(jnp.float32) * rows[peer, k, r].astype(jnp.float32)
                for j in range(height // 8):
                    total += product[8 * j : 8 * j + 8]
            sums[a, b] = jnp.sum(total, axis=0)
        return carry

    lax.fori_loop(0, 2 * count * rx_peers, dots, 0)
    ones = jnp.ones((8, breadth), jnp.float32)
    wide = 2 * count * rx_peers
    line_sums[column] = jnp.zeros(line_sums.shape[1:], jnp.float32)
    for a in range(2 * count):
        lanes = lax.dot_general(
            ones,
            sums[a],
            (((1,), (1,)), ((), ())),
            precision=lax.Precision.HIGHEST,
            preferred_element_type=jnp.float32,
        )
        line_sums[column, a : a + 1, 0:wide] = lanes[0:1]

    step_one = [
        pltpu.make_async_remote_copy(
            line_sums.at[column],
            line_sums.at[column],
            ssend_sem.at[0, k],
            srecv_sem.at[0, k],
            device_id=target,
            device_id_type=MESH,
        )
        for k, target in enumerate(along)
    ]
    for copy in step_one:
        copy.start()
    for copy in step_one:
        copy.wait_recv()
    plane_sums[line] = jnp.sum(line_sums[...], axis=0)
    step_two = [
        pltpu.make_async_remote_copy(
            plane_sums.at[line],
            plane_sums.at[line],
            ssend_sem.at[1, k],
            srecv_sem.at[1, k],
            device_id=target,
            device_id_type=MESH,
        )
        for k, target in enumerate(across)
    ]
    for copy in step_two:
        copy.start()
    for copy in step_two:
        copy.wait_recv()
    total = jnp.sum(plane_sums[...], axis=0)
    cells = depth * height * breadth * peers
    block_ref[...] = total[0 : 2 * count, 0:wide] / cells
    for copy in copies + ccopies + halo + gather + step_one + step_two:
        copy.wait_send()
    out.wait()


def shards(conductivity, background, warm_start, data_weight, recv_cell, src_group, group_freq):
    count = warm_start.shape[0]
    depth, height, breadth = conductivity.shape
    peers, rx_peers = lax.axis_size("space"), lax.axis_size("rx")
    lines = 1
    while lines * lines < peers:
        lines *= 2
    columns = peers // lines
    rows = 2 * count
    wide = rows * rx_peers
    plane = (height, breadth)
    f32, b16 = jnp.float32, jnp.bfloat16
    vmem, dma = pltpu.VMEM, pltpu.SemaphoreType.DMA
    hbm = pl.BlockSpec(memory_space=pltpu.HBM)
    block, smoothed = pl.pallas_call(
        functools.partial(kernel, peers, lines, rx_peers),
        name="inversion_step",
        out_shape=(
            jax.ShapeDtypeStruct((rows, wide), f32),
            jax.ShapeDtypeStruct((rows, depth) + plane, b16),
        ),
        in_specs=[hbm] * 7,
        out_specs=(pl.BlockSpec(memory_space=vmem), hbm),
        scratch_shapes=[
            vmem(conductivity.shape, f32),
            vmem(background.shape, f32),
            vmem(warm_start.shape, f32),
            pltpu.SMEM(data_weight.shape, f32),
            pltpu.SMEM(recv_cell.shape, jnp.int32),
            pltpu.SMEM(src_group.shape, jnp.int32),
            pltpu.SMEM(group_freq.shape, jnp.int32),
            vmem((depth, 3, rows) + plane, b16),
            vmem((depth,) + plane, b16),
            vmem((2, depth, 3, rows) + plane, b16),
            vmem((2, depth) + plane, b16),
            vmem((rows, 3, 3 * depth) + plane, f32),
            vmem((rows, 3, 3 * depth) + plane, f32),
            vmem((rows, 3, 3 * depth) + plane, f32),
            vmem((rx_peers, depth, rows) + plane, b16),
            vmem((2, 2, rows) + plane, b16),
            vmem((rows, depth) + plane, b16),
            vmem((rows, wide, breadth), f32),
            vmem((columns, 8, 128), f32),
            vmem((lines, 8, 128), f32),
            dma((7,)),
            dma,
            dma((2, depth + 1)),
            dma((2, depth + 1)),
            dma((2,)),
            dma((2,)),
            dma((rx_peers - 1,)),
            dma((rx_peers - 1,)),
            dma((2, max(lines, columns) - 1)),
            dma((2, max(lines, columns) - 1)),
        ],
        compiler_params=pltpu.CompilerParams(
            collective_id=0, has_side_effects=True, vmem_limit_bytes=48 * 2**20
        ),
    )(conductivity, background, warm_start, data_weight, recv_cell, src_group, group_freq)
    return block, smoothed.reshape((count, 2, depth) + plane)


def solution(mesh):
    in_specs = (
        P("space", None, None),
        P(None, None, None, "space", None, None),
        P("rx", None, None, "space", None, None),
        P("rx", None, None),
        P("rx"),
        P("rx"),
        P(),
    )
    out_specs = (P("rx", None), P("rx", None, "space", None, None))
    return jax.shard_map(shards, mesh=mesh, in_specs=in_specs, out_specs=out_specs, check_vma=False)
```

time: 722 us -> 65.6 us (0.09)
  the two profiles are of different devices: /device:TPU:6 before, /device:TPU:1 now
where the time goes in v1:
time: 65.6 us; the launch traced here: 65.3 us
  Pallas kernels  57.6 us (88%)
  local copies, waits for them, and re-layouts  6.99 us (11%)
  between operations  0.66 us (1%)
    pallas_call x1, Pallas kernels, shards(): pl.pallas_call(functools.partial(kernel, peers, lines, rx_peers), name='i...  57.6 us
    unnamed x16, local copies, waits for them, and re-layouts  6.99 us

profile of v1, /device:TPU:1, one launch (start us, length us, event | category | flops | bytes accessed | tf_op | source)
XLA Modules:
  0.0 65.3 jit_solution(896731135847284080)
XLA Ops:
  0.6 0.0 copy-start
  0.6 1.3 %copy-done = f32[4,2,3,3,32,128]{5,4,3,2,1,0:T(8,128)S(1)} copy-done((f32[4,2,3,3,32,128]{5,4,3,2,1,0:T(8,128)S(1)}, f32[4,2,3,3,32,128]{5,4,3,2,1,0:T(8,128)}, u32[]{:S(2)}) %copy-start) | copy-done | bytes 1179672
  1.9 0.0 copy-start.1
  1.9 1.1 %copy-done.1 = f32[2,2,3,3,32,128]{5,4,3,2,1,0:T(8,128)S(1)} copy-done((f32[2,2,3,3,32,128]{5,4,3,2,1,0:T(8,128)S(1)}, f32[2,2,3,3,32,128]{5,4,3,2,1,0:T(8,128)}, u32[]{:S(2)}) %copy-start.1) | copy-done | bytes 589848
  3.0 0.0 copy-start.2
  3.0 0.8 %copy-done.2 = f32[3,32,128]{2,1,0:T(8,128)S(1)} copy-done((f32[3,32,128]{2,1,0:T(8,128)S(1)}, f32[3,32,128]{2,1,0:T(8,128)}, u32[]{:S(2)}) %copy-start.2) | copy-done | bytes 49176
  3.8 0.0 copy-start.3
  3.8 0.7 %copy-done.3 = f32[2,2,3]{2,1,0:T(2,128)S(1)} copy-done((f32[2,2,3]{2,1,0:T(2,128)S(1)}, f32[2,2,3]{2,1,0:T(2,128)}, u32[]{:S(2)}) %copy-start.3) | copy-done | bytes 72
  4.4 0.0 copy-start.4
  4.5 0.7 %copy-done.4 = s32[2]{0:T(128)S(1)} copy-done((s32[2]{0:T(128)S(1)}, s32[2]{0:T(128)}, u32[]{:S(2)}) %copy-start.4) | copy-done | bytes 32
  5.1 0.0 copy-start.5
  5.1 0.7 %copy-done.5 = s32[2]{0:T(128)S(1)} copy-done((s32[2]{0:T(128)S(1)}, s32[2]{0:T(128)}, u32[]{:S(2)}) %copy-start.5) | copy-done | bytes 32
  5.8 0.0 copy-start.6
  5.8 0.7 %copy-done.6 = s32[4]{0:T(128)S(1)} copy-done((s32[4]{0:T(128)S(1)}, s32[4]{0:T(128)}, u32[]{:S(2)}) %copy-start.6) | copy-done | bytes 40
  6.4 57.6 %inversion_step.1 = (f32[4,16]{1,0:T(4,128)S(1)}, bf16[4,3,32,128]{3,2,1,0:T(8,128)(2,1)S(1)}) custom-call(f32[3,32,128]{2,1,0:T(8,128)S(1)} %copy-done.2, f32[4,2,3,3,32,128]{5,4,3,2,1,0:T(8,128)S(1)} %copy-done, f32[2,2,3,3,32,128]{5,4,3,2,1,0:T(8,128)S(1)} %copy-done.1, f32[2,2,3]{2,1,0:T(2,128)S(1)} %copy-done.3, s32[2]{0:T(128)S(1)} %copy-done.4, ...), custom_call_target="tpu_custom_call" | custom-call | tf_op jit(solution)/shard_map/inversion_step/pallas_call | solution.py:394
  64.0 0.6 copy.11
  64.6 0.6 copy.12
Async XLA Ops:
  0.6 1.3 %copy-start = (f32[4,2,3,3,32,128]{5,4,3,2,1,0:T(8,128)S(1)}, f32[4,2,3,3,32,128]{5,4,3,2,1,0:T(8,128)}, u32[]{:S(2)}) copy-start(f32[4,2,3,3,32,128]{5,4,3,2,1,0:T(8,128)} %back_hbm.1) | copy-start | bytes 3538948
  1.9 1.1 %copy-start.1 = (f32[2,2,3,3,32,128]{5,4,3,2,1,0:T(8,128)S(1)}, f32[2,2,3,3,32,128]{5,4,3,2,1,0:T(8,128)}, u32[]{:S(2)}) copy-start(f32[2,2,3,3,32,128]{5,4,3,2,1,0:T(8,128)} %warm_hbm.1) | copy-start | bytes 1769476
  3.0 0.8 %copy-start.2 = (f32[3,32,128]{2,1,0:T(8,128)S(1)}, f32[3,32,128]{2,1,0:T(8,128)}, u32[]{:S(2)}) copy-start(f32[3,32,128]{2,1,0:T(8,128)} %cond_hbm.1) | copy-start | bytes 147460
  3.8 0.7 %copy-start.3 = (f32[2,2,3]{2,1,0:T(2,128)S(1)}, f32[2,2,3]{2,1,0:T(2,128)}, u32[]{:S(2)}) copy-start(f32[2,2,3]{2,1,0:T(2,128)} %weight_hbm.1) | copy-start | bytes 148
  4.4 0.7 %copy-start.4 = (s32[2]{0:T(128)S(1)}, s32[2]{0:T(128)}, u32[]{:S(2)}) copy-start(s32[2]{0:T(128)} %cell_hbm.1) | copy-start | bytes 28
  5.1 0.7 %copy-start.5 = (s32[2]{0:T(128)S(1)}, s32[2]{0:T(128)}, u32[]{:S(2)}) copy-start(s32[2]{0:T(128)} %group_hbm.1) | copy-start | bytes 28
  5.8 0.7 %copy-start.6 = (s32[4]{0:T(128)S(1)}, s32[4]{0:T(128)}, u32[]{:S(2)}) copy-start(s32[4]{0:T(128)} %freq_hbm.1) | copy-start | bytes 52

commit v2 on v1

--- a/solution.py
+++ b/solution.py
@@ -25,7 +25,7 @@
     group_hbm,
     freq_hbm,
     block_ref,
-    smooth_hbm,
+    smooth,
     cond,
     back,
     warm,
@@ -34,6 +34,7 @@
     group,
     freq,
     send,
+    mix,
     csend,
     land,
     cland,
@@ -42,12 +43,10 @@
     third,
     rows,
     rland,
-    smooth,
     sums,
     line_sums,
     plane_sums,
     load_sem,
-    out_sem,
     send_sem,
     recv_sem,
     rsend_sem,
@@ -56,6 +55,7 @@
     grecv_sem,
     ssend_sem,
     srecv_sem,
+    meet_sem,
 ):
     depth = cond.shape[0]
     height, breadth = cond.shape[1:]
@@ -68,8 +68,19 @@
     after = (rx, (me + 1) % peers)
     before = (rx, (me + peers - 1) % peers)
     others = [((rx + k) % rx_peers, me) for k in range(1, rx_peers)]
-    along = [(rx, line * columns + (column + k) % columns) for k in range(1, columns)]
-    across = [(rx, ((line + k) % lines) * columns + column) for k in range(1, lines)]
+
+    def at(line, column):
+        return (rx, (line % lines) * columns + column % columns)
+
+    along = [at(line, column + k) for k in range(1, columns)]
+    across = [at(line + k, column) for k in range(1, lines)]
+    rows_y = lines // 2
+    half = (line // rows_y) * rows_y
+
+    def beside(k):
+        return at(half + (line + k + rows_y) % rows_y, column)
+
+    opposite = at(line + rows_y, column)
 
     loads = [
         pltpu.make_async_copy(src, dst, load_sem.at[i])
@@ -88,71 +99,109 @@
     for load in loads:
         load.start()
     barrier = pltpu.get_barrier_semaphore()
-    partners = [before, after] + others + along + across
+    near = [at(line, column + 1), at(line, column - 1), opposite]
+    if rows_y > 1:
+        near += [beside(1), beside(-1)]
+    partners = [before, after] + near + others
     for partner in partners:
         pl.semaphore_signal(barrier, inc=1, device_id=partner, device_id_type=MESH)
+
+    meetings = []
+    reach, y_steps = 1, 0
+    while reach < max(columns, rows_y) // 2:
+        targets = []
+        if reach < columns // 2:
+            targets += [at(line, column + reach), at(line, column - reach)]
+        if reach < rows_y // 2:
+            targets += [beside(reach), beside(-reach)]
+            y_steps += 1
+        meetings.append(targets)
+        reach *= 2
+    if len(meetings) == y_steps:
+        meetings.append([])
+    meetings[y_steps].append(opposite)
+    taken = []
+
+    def meet(steps):
+        while len(taken) < min(steps, len(meetings) + 1):
+            step = len(taken)
+            if step > 0:
+                pl.semaphore_wait(meet_sem.at[step - 1], len(meetings[step - 1]))
+            if step < len(meetings):
+                for target in meetings[step]:
+                    pl.semaphore_signal(
+                        meet_sem.at[step], inc=1, device_id=target, device_id_type=MESH
+                    )
+            taken.append(step)
 
     for load in loads[:2]:
         load.wait()
     csend[...] = cond[...].astype(jnp.bfloat16)
-
-    def pack(s, carry):
-        for p in range(2):
+    iy = lax.broadcasted_iota(jnp.int32, (height, breadth), 0)
+    iz = lax.broadcasted_iota(jnp.int32, (height, breadth), 1)
+    flat = iy * breadth + iz
+
+    def y_up(f):
+        return jnp.where(iy == height - 1, 0.0, pltpu.roll(f, height - 1, 0))
+
+    def y_down(f):
+        return jnp.where(iy == 0, 0.0, pltpu.roll(f, 1, 0))
+
+    def z_up(f):
+        return jnp.where(iz == breadth - 1, 0.0, pltpu.roll(f, breadth - 1, 1))
+
+    def z_down(f):
+        return jnp.where(iz == 0, 0.0, pltpu.roll(f, 1, 1))
+
+    def pack(i, carry):
+        s, p = i // 2, i % 2
+        for plane in range(depth):
             for c in range(3):
-                send[:, c, 2 * s + p] = warm[s, p, c].astype(jnp.bfloat16)
+                send[plane, c, i] = warm[s, p, c, plane].astype(jnp.bfloat16)
+        ex = warm[s, p, 0, 0]
+        mix[0, i] = (warm[s, p, 1, 0] + (y_up(ex) - ex)).astype(jnp.bfloat16)
+        mix[1, i] = (warm[s, p, 2, 0] + (z_up(ex) - ex)).astype(jnp.bfloat16)
         return carry
 
-    lax.fori_loop(0, count, pack, 0)
+    lax.fori_loop(0, 2 * count, pack, 0)
     pl.semaphore_wait(barrier, len(partners))
 
-    copies = []
-    for k in range(depth):
-        for way, target in ((0, after), (1, before)):
-            plane = depth - 1 - k if way == 0 else k
-            copies.append(
-                pltpu.make_async_remote_copy(
-                    send.at[plane],
-                    land.at[way, plane],
-                    send_sem.at[way, k],
-                    recv_sem.at[way, k],
-                    device_id=target,
-                    device_id_type=MESH,
-                )
-            )
-    ccopies = [
-        pltpu.make_async_remote_copy(
-            csend,
-            cland.at[way],
-            send_sem.at[way, depth],
-            recv_sem.at[way, depth],
+    def halo(k, way, target, source, place):
+        return pltpu.make_async_remote_copy(
+            source,
+            place,
+            send_sem.at[way, k],
+            recv_sem.at[way, k],
             device_id=target,
             device_id_type=MESH,
         )
-        for way, target in ((0, after), (1, before))
-    ]
-    for copy in copies[:2] + ccopies + copies[2:]:
-        copy.start()
+
+    last = depth - 1
+    far = [
+        halo(last, 0, after, mix, land.at[0, 0, pl.ds(1, 2)]),
+        halo(last, 1, before, send.at[last, pl.ds(1, 2)], land.at[1, last, pl.ds(1, 2)]),
+    ]
+    inner = [
+        [
+            halo(k, 0, after, send.at[last - k], land.at[0, last - k]),
+            halo(k, 1, before, send.at[k], land.at[1, k]),
+        ]
+        for k in range(last)
+    ]
+    coefs = [
+        halo(depth, 0, after, csend.at[pl.ds(1, last)], cland.at[0, pl.ds(1, last)]),
+        halo(depth, 1, before, csend.at[pl.ds(0, last)], cland.at[1, pl.ds(0, last)]),
+    ]
+    stages = [inner[0] + coefs] + inner[1:] + [far]
+    for stage in stages:
+        for copy in stage:
+            copy.start()
+    meet(1)
 
     for load in loads[2:]:
         load.wait()
     has_before = (me > 0).astype(jnp.float32)
     has_after = (me < peers - 1).astype(jnp.float32)
-    iy = lax.broadcasted_iota(jnp.int32, (height, breadth), 0)
-    iz = lax.broadcasted_iota(jnp.int32, (height, breadth), 1)
-    flat = iy * breadth + iz
-
-    def y_up(f):
-        return jnp.where(iy == height - 1, 0.0, pltpu.roll(f, height - 1, 0))
-
-    def y_down(f):
-        return jnp.where(iy == 0, 0.0, pltpu.roll(f, 1, 0))
-
-    def z_up(f):
-        return jnp.where(iz == breadth - 1, 0.0, pltpu.roll(f, breadth - 1, 1))
-
-    def z_down(f):
-        return jnp.where(iz == 0, 0.0, pltpu.roll(f, 1, 1))
-
     def angular_of(s):
         k = freq[group[s]]
         low = jnp.where(k % 2 == 1, jnp.float32(1.25), jnp.float32(1.0))
@@ -184,25 +233,32 @@
     def stored(buffer):
         return lambda s, p, c, plane: buffer[2 * s + p, c, plane]
 
-    def sweep(source, target, low, high):
+    def sweep(source, target, *spans):
         def one(i, carry):
             s, p = i // 2, i % 2
             turn = (1 - 2 * p).astype(jnp.float32) * (RELAX * angular_of(s))
+            for low, high in spans:
+                span(s, p, i, turn, low, high)
+            return carry
+
+        def span(s, p, i, turn, low, high):
             old = {
                 (c, plane): source(s, p, c, plane)
                 for plane in range(low - 1, high + 1)
                 for c in range(3)
+                if plane not in (0, 3 * depth - 1) or c > 0
             }
 
             def mag_y(plane):
-                ex = old[0, plane]
-                return (z_up(ex) - ex) - (old[2, plane + 1] - old[2, plane])
+                return (z_up(old[0, plane]) - old[0, plane]) - (old[2, plane + 1] - old[2, plane])
 
             def mag_z(plane):
-                ex = old[0, plane]
-                return (old[1, plane + 1] - old[1, plane]) - (y_up(ex) - ex)
-
-            hy_low, hz_low = mag_y(low - 1), mag_z(low - 1)
+                return (old[1, plane + 1] - old[1, plane]) - (y_up(old[0, plane]) - old[0, plane])
+
+            if low == 1:
+                hy_low, hz_low = old[2, 0] - old[2, 1], old[1, 1] - old[1, 0]
+            else:
+                hy_low, hz_low = mag_y(low - 1), mag_z(low - 1)
             for plane in range(low, high):
                 ey, ez = old[1, plane], old[2, plane]
                 hx = (y_up(ez) - ez) - (z_up(ey) - ey)
@@ -221,16 +277,29 @@
                     term = jnp.where(point, RELAX * weight[s, p, c], 0.0)
                     new = old[c, plane] + term - RELAX * curl[c] + factor * other
                     target[i, c, plane] = guard(plane, new)
-            return carry
 
         lax.fori_loop(0, 2 * count, one, 0)
 
-    own = (depth, 2 * depth)
-    for copy in copies + ccopies:
-        copy.wait_recv()
-    sweep(start_plane, first, own[0] - 2, own[1] + 2)
-    sweep(stored(first), second, own[0] - 1, own[1] + 1)
-    sweep(stored(second), third, own[0], own[1])
+    iterates = [start_plane, stored(first), stored(second), stored(third)]
+    buffers = [None, first, second, third]
+    if depth > 2:
+        sweep(iterates[0], buffers[1], (depth + 1, 2 * depth - 1))
+    for k, stage in enumerate(stages):
+        for copy in stage:
+            copy.wait_recv()
+        for it in range(1, k + 2):
+            reached = k + 1 - it
+            low, high = depth - reached, 2 * depth + reached
+            if it == k + 1:
+                inside = (low + 1, high - 1) if it == 1 and depth > 2 else None
+                if inside is None:
+                    sweep(iterates[it - 1], buffers[it], (low, high))
+                else:
+                    sweep(iterates[it - 1], buffers[it], (low, low + 1), (high - 1, high))
+            else:
+                sweep(iterates[it - 1], buffers[it], (low, low + 1), (high - 1, high))
+
+    meet(2)
 
     def products(s, carry):
         g = group[s]
@@ -250,7 +319,7 @@
 
     lax.fori_loop(0, count, products, 0)
 
-    halo = [
+    edges = [
         pltpu.make_async_remote_copy(
             rows.at[rx, pl.ds(start, 2)],
             rland.at[way],
@@ -272,9 +341,10 @@
         )
         for k, target in enumerate(others)
     ]
-    for copy in halo + gather:
+    for copy in gather + edges:
         copy.start()
-    for copy in halo:
+    meet(len(meetings))
+    for copy in edges:
         copy.wait_recv()
 
     def smoothing(r, carry):
@@ -307,8 +377,6 @@
         return carry
 
     lax.fori_loop(0, 2 * count, smoothing, 0)
-    out = pltpu.make_async_copy(smooth, smooth_hbm, out_sem)
-    out.start()
 
     for copy in gather:
         copy.wait_recv()
@@ -349,6 +417,7 @@
         )
         for k, target in enumerate(along)
     ]
+    meet(len(meetings) + 1)
     for copy in step_one:
         copy.start()
     for copy in step_one:
@@ -372,9 +441,8 @@
     total = jnp.sum(plane_sums[...], axis=0)
     cells = depth * height * breadth * peers
     block_ref[...] = total[0 : 2 * count, 0:wide] / cells
-    for copy in copies + ccopies + halo + gather + step_one + step_two:
+    for copy in sum(stages, []) + edges + gather + step_one + step_two:
         copy.wait_send()
-    out.wait()
 
 
 def shards(conductivity, background, warm_start, data_weight, recv_cell, src_group, group_freq):
@@ -391,15 +459,25 @@
     f32, b16 = jnp.float32, jnp.bfloat16
     vmem, dma = pltpu.VMEM, pltpu.SemaphoreType.DMA
     hbm = pl.BlockSpec(memory_space=pltpu.HBM)
+    operands = (
+        conductivity,
+        background,
+        warm_start,
+        data_weight,
+        recv_cell,
+        src_group,
+        group_freq,
+    )
+    pinned = [pltpu.with_memory_space_constraint(x, pltpu.HBM) for x in operands]
     block, smoothed = pl.pallas_call(
         functools.partial(kernel, peers, lines, rx_peers),
         name="inversion_step",
         out_shape=(
-            jax.ShapeDtypeStruct((rows, wide), f32),
-            jax.ShapeDtypeStruct((rows, depth) + plane, b16),
+            pltpu.VMEM((rows, wide), f32),
+            pltpu.VMEM((rows, depth) + plane, b16),
         ),
         in_specs=[hbm] * 7,
-        out_specs=(pl.BlockSpec(memory_space=vmem), hbm),
+        out_specs=(pl.BlockSpec(memory_space=vmem), pl.BlockSpec(memory_space=vmem)),
         scratch_shapes=[
             vmem(conductivity.shape, f32),
             vmem(background.shape, f32),
@@ -409,6 +487,7 @@
             pltpu.SMEM(src_group.shape, jnp.int32),
             pltpu.SMEM(group_freq.shape, jnp.int32),
             vmem((depth, 3, rows) + plane, b16),
+            vmem((2, rows) + plane, b16),
             vmem((depth,) + plane, b16),
             vmem((2, depth, 3, rows) + plane, b16),
             vmem((2, depth) + plane, b16),
@@ -417,12 +496,10 @@
             vmem((rows, 3, 3 * depth) + plane, f32),
             vmem((rx_peers, depth, rows) + plane, b16),
             vmem((2, 2, rows) + plane, b16),
-            vmem((rows, depth) + plane, b16),
             vmem((rows, wide, breadth), f32),
             vmem((columns, 8, 128), f32),
             vmem((lines, 8, 128), f32),
             dma((7,)),
-            dma,
             dma((2, depth + 1)),
             dma((2, depth + 1)),
             dma((2,)),
@@ -431,11 +508,12 @@
             dma((rx_peers - 1,)),
             dma((2, max(lines, columns) - 1)),
             dma((2, max(lines, columns) - 1)),
+            pltpu.SemaphoreType.REGULAR((4,)),
         ],
         compiler_params=pltpu.CompilerParams(
             collective_id=0, has_side_effects=True, vmem_limit_bytes=48 * 2**20
         ),
-    )(conductivity, background, warm_start, data_weight, recv_cell, src_group, group_freq)
+    )(*pinned)
     return block, smoothed.reshape((count, 2, depth) + plane)
 
 

time: 65.6 us -> 52.4 us (0.80)
  the two profiles are of different devices: /device:TPU:1 before, /device:TPU:4 now
where the time goes in v2:
time: 52.4 us; the launch traced here: 52.2 us
  Pallas kernels  50.3 us (96%)
  local copies, waits for them, and re-layouts  1.22 us (2%)
  between operations  0.64 us (1%)
    pallas_call x1, Pallas kernels, shards(): pl.pallas_call(functools.partial(kernel, peers, lines, rx_peers), name='i...  50.3 us
    unnamed x2, local copies, waits for them, and re-layouts  1.22 us

profile of v2, /device:TPU:4, one launch (start us, length us, event | category | flops | bytes accessed | tf_op | source)
XLA Modules:
  0.0 52.2 jit_solution(9469585849383351470)
XLA Ops:
  0.6 50.3 %inversion_step.1 = (f32[4,16]{1,0:T(4,128)S(1)}, bf16[4,3,32,128]{3,2,1,0:T(8,128)(2,1)S(1)}) custom-call(f32[3,32,128]{2,1,0:T(8,128)} %cond_hbm.1, f32[4,2,3,3,32,128]{5,4,3,2,1,0:T(8,128)} %back_hbm.1, f32[2,2,3,3,32,128]{5,4,3,2,1,0:T(8,128)} %warm_hbm.1, f32[2,2,3]{2,1,0:T(2,128)} %weight_hbm.1, s32[2]{0:T(128)} %cell_hbm.1, s32[2]{0:T(128)} %group_hbm.1, ...), custom_call_target="tpu_custom_call" | custom-call | tf_op jit(solution)/shard_map/inversion_step/pallas_call | solution.py:472
  51.0 0.6 %copy.11 = f32[4,16]{1,0:T(4,128)} copy(f32[4,16]{1,0:T(4,128)S(1)} %get-tuple-element.6) | data formatting | bytes 512
  51.6 0.6 %copy.12 = bf16[2,2,3,32,128]{4,3,2,1,0:T(8,128)(2,1)} copy(bf16[2,2,3,32,128]{4,3,2,1,0:T(8,128)(2,1)S(1)} %bitcast.1) | data formatting | bytes 196608

commit v3 on v2

--- a/solution.py
+++ b/solution.py
@@ -34,13 +34,17 @@
     group,
     freq,
     send,
-    mix,
-    csend,
     land,
     cland,
-    first,
-    second,
-    third,
+    alone_1,
+    alone_2,
+    alone_3,
+    delta_1,
+    delta_2,
+    delta_3,
+    echo,
+    reply,
+    extra,
     rows,
     rland,
     sums,
@@ -136,7 +140,6 @@
 
     for load in loads[:2]:
         load.wait()
-    csend[...] = cond[...].astype(jnp.bfloat16)
     iy = lax.broadcasted_iota(jnp.int32, (height, breadth), 0)
     iz = lax.broadcasted_iota(jnp.int32, (height, breadth), 1)
     flat = iy * breadth + iz
@@ -153,49 +156,36 @@
     def z_down(f):
         return jnp.where(iz == 0, 0.0, pltpu.roll(f, 1, 1))
 
+    def outflow(k, i, first_plane, last_plane):
+        ex, ey, ez = last_plane
+        send[k, 0, 0, i] = (ey + (y_up(ex) - ex)).astype(jnp.bfloat16)
+        send[k, 0, 1, i] = (ez + (z_up(ex) - ex)).astype(jnp.bfloat16)
+        send[k, 1, 0, i] = first_plane[1].astype(jnp.bfloat16)
+        send[k, 1, 1, i] = first_plane[2].astype(jnp.bfloat16)
+
     def pack(i, carry):
         s, p = i // 2, i % 2
-        for plane in range(depth):
-            for c in range(3):
-                send[plane, c, i] = warm[s, p, c, plane].astype(jnp.bfloat16)
-        ex = warm[s, p, 0, 0]
-        mix[0, i] = (warm[s, p, 1, 0] + (y_up(ex) - ex)).astype(jnp.bfloat16)
-        mix[1, i] = (warm[s, p, 2, 0] + (z_up(ex) - ex)).astype(jnp.bfloat16)
-        return carry
-
-    lax.fori_loop(0, 2 * count, pack, 0)
+        outflow(0, i, [warm[s, p, c, 0] for c in range(3)], [warm[s, p, c, last] for c in range(3)])
+        return carry
+
+    last = depth - 1
+    lax.fori_loop(0, 2 * count, pack, 0, unroll=2)
     pl.semaphore_wait(barrier, len(partners))
 
-    def halo(k, way, target, source, place):
+    def halo(k, way, source, place):
         return pltpu.make_async_remote_copy(
             source,
             place,
             send_sem.at[way, k],
             recv_sem.at[way, k],
-            device_id=target,
+            device_id=(after, before)[way],
             device_id_type=MESH,
         )
 
-    last = depth - 1
-    far = [
-        halo(last, 0, after, mix, land.at[0, 0, pl.ds(1, 2)]),
-        halo(last, 1, before, send.at[last, pl.ds(1, 2)], land.at[1, last, pl.ds(1, 2)]),
-    ]
-    inner = [
-        [
-            halo(k, 0, after, send.at[last - k], land.at[0, last - k]),
-            halo(k, 1, before, send.at[k], land.at[1, k]),
-        ]
-        for k in range(last)
-    ]
-    coefs = [
-        halo(depth, 0, after, csend.at[pl.ds(1, last)], cland.at[0, pl.ds(1, last)]),
-        halo(depth, 1, before, csend.at[pl.ds(0, last)], cland.at[1, pl.ds(0, last)]),
-    ]
-    stages = [inner[0] + coefs] + inner[1:] + [far]
-    for stage in stages:
-        for copy in stage:
-            copy.start()
+    flows = [[halo(k, way, send.at[k, way], land.at[k, way]) for way in (0, 1)] for k in range(ITERS)]
+    coefs = [halo(ITERS, 0, cond.at[last], cland.at[0]), halo(ITERS, 1, cond.at[0], cland.at[1])]
+    for copy in flows[0] + coefs:
+        copy.start()
     meet(1)
 
     for load in loads[2:]:
@@ -209,6 +199,13 @@
         top = jnp.where((k // 4) % 2 == 1, jnp.float32(1.25**4), jnp.float32(1.0))
         return 0.25 * (low * mid * top)
 
+    def angular_of(s):
+        k = freq[group[s]]
+        low = jnp.where(k % 2 == 1, jnp.float32(1.25), jnp.float32(1.0))
+        mid = jnp.where((k // 2) % 2 == 1, jnp.float32(1.25**2), jnp.float32(1.0))
+        top = jnp.where((k // 4) % 2 == 1, jnp.float32(1.25**4), jnp.float32(1.0))
+        return 0.25 * (low * mid * top)
+
     def guard(plane, f):
         if plane < depth:
             return f * has_before
@@ -230,118 +227,228 @@
             return cland[1, plane - 2 * depth].astype(jnp.float32)
         return cond[plane - depth]
 
-    def stored(buffer):
-        return lambda s, p, c, plane: buffer[2 * s + p, c, plane]
-
-    def sweep(source, target, *spans):
+    def inflow_low(first_part, second_part, weight_):
+        return (0.0, weight_ * first_part, weight_ * second_part)
+
+    def inflow_high(ey, ez, weight_):
+        div = (ey - y_down(ey)) + (ez - z_down(ez))
+        return (-weight_ * div, weight_ * ey, weight_ * ez)
+
+    def step(s, p, old, other, coef, with_source):
+        turn = (1 - 2 * p).astype(jnp.float32) * (RELAX * angular_of(s))
+        planes = len(old)
+        hy_low, hz_low = -old[0][2], old[0][1]
+        new = []
+        for plane in range(planes):
+            ex, ey, ez = old[plane]
+            hx = (y_up(ez) - ez) - (z_up(ey) - ey)
+            hy = (z_up(ex) - ex) + ez
+            hz = (ex - y_up(ex)) - ey
+            if plane < planes - 1:
+                hy = hy - old[plane + 1][2]
+                hz = hz + old[plane + 1][1]
+            curl = (
+                (hz - y_down(hz)) - (hy - z_down(hy)),
+                (hx - z_down(hx)) - (hz - hz_low),
+                (hy - hy_low) - (hx - y_down(hx)),
+            )
+            hy_low, hz_low = hy, hz
+            factor = turn * coef(plane)
+            fresh = [old[plane][c] - RELAX * curl[c] + factor * other(c, plane) for c in range(3)]
+            if with_source:
+                point = flat == cell[s] - (me * depth + plane) * (height * breadth)
+                fresh = [
+                    fresh[c] + jnp.where(point, RELAX * weight[s, p, c], 0.0) for c in range(3)
+                ]
+            new.append(fresh)
+        return new
+
+    def from_warm(i, c, plane):
+        return warm[i // 2, i % 2, c, plane]
+
+    def held(buffer):
+        return lambda i, c, plane: buffer[i, c, plane]
+
+    def sweep(source, target, with_source, send_slot=None):
         def one(i, carry):
             s, p = i // 2, i % 2
-            turn = (1 - 2 * p).astype(jnp.float32) * (RELAX * angular_of(s))
-            for low, high in spans:
-                span(s, p, i, turn, low, high)
+            old = [[source(i, c, plane) for c in range(3)] for plane in range(depth)]
+            twin = i + 1 - 2 * p
+            new = step(
+                s, p, old, lambda c, plane: source(twin, c, plane), lambda k: cond[k], with_source
+            )
+            for plane in range(depth):
+                for c in range(3):
+                    target[i, c, plane] = new[plane][c]
+            if send_slot is not None:
+                outflow(send_slot, i, new[0], new[last])
             return carry
 
-        def span(s, p, i, turn, low, high):
-            old = {
-                (c, plane): source(s, p, c, plane)
-                for plane in range(low - 1, high + 1)
-                for c in range(3)
-                if plane not in (0, 3 * depth - 1) or c > 0
-            }
-
-            def mag_y(plane):
-                return (z_up(old[0, plane]) - old[0, plane]) - (old[2, plane + 1] - old[2, plane])
-
-            def mag_z(plane):
-                return (old[1, plane + 1] - old[1, plane]) - (y_up(old[0, plane]) - old[0, plane])
-
-            if low == 1:
-                hy_low, hz_low = old[2, 0] - old[2, 1], old[1, 1] - old[1, 0]
-            else:
-                hy_low, hz_low = mag_y(low - 1), mag_z(low - 1)
-            for plane in range(low, high):
-                ey, ez = old[1, plane], old[2, plane]
-                hx = (y_up(ez) - ez) - (z_up(ey) - ey)
-                hy, hz = mag_y(plane), mag_z(plane)
-                curl = (
-                    (hz - y_down(hz)) - (hy - z_down(hy)),
-                    (hx - z_down(hx)) - (hz - hz_low),
-                    (hy - hy_low) - (hx - y_down(hx)),
-                )
-                hy_low, hz_low = hy, hz
-                factor = turn * cond_plane(plane)
-                here = cell[s] - (me * depth + plane - depth) * (height * breadth)
-                point = flat == here
-                for c in range(3):
-                    other = source(s, 1 - p, c, plane)
-                    term = jnp.where(point, RELAX * weight[s, p, c], 0.0)
-                    new = old[c, plane] + term - RELAX * curl[c] + factor * other
-                    target[i, c, plane] = guard(plane, new)
-
-        lax.fori_loop(0, 2 * count, one, 0)
-
-    iterates = [start_plane, stored(first), stored(second), stored(third)]
-    buffers = [None, first, second, third]
-    if depth > 2:
-        sweep(iterates[0], buffers[1], (depth + 1, 2 * depth - 1))
-    for k, stage in enumerate(stages):
-        for copy in stage:
-            copy.wait_recv()
-        for it in range(1, k + 2):
-            reached = k + 1 - it
-            low, high = depth - reached, 2 * depth + reached
-            if it == k + 1:
-                inside = (low + 1, high - 1) if it == 1 and depth > 2 else None
-                if inside is None:
-                    sweep(iterates[it - 1], buffers[it], (low, high))
-                else:
-                    sweep(iterates[it - 1], buffers[it], (low, low + 1), (high - 1, high))
-            else:
-                sweep(iterates[it - 1], buffers[it], (low, low + 1), (high - 1, high))
-
+        lax.fori_loop(0, 2 * count, one, 0, unroll=2)
+
+    sweep(from_warm, alone_1, True, 1)
+    for copy in flows[1]:
+        copy.start()
+    sweep(held(alone_1), alone_2, True, 2)
+    for copy in flows[2]:
+        copy.start()
+    sweep(held(alone_2), alone_3, True)
+
+    def answer(i, carry):
+        first_plane = [from_warm(i, c, 0) for c in range(3)]
+        ex, ey, ez = [from_warm(i, c, last) for c in range(3)]
+        low = inflow_high(first_plane[1], first_plane[2], RELAX)
+        high = inflow_low(ey + (y_up(ex) - ex), ez + (z_up(ex) - ex), RELAX)
+        echo[0, i, 0], echo[0, i, 1], echo[0, i, 2] = low
+        echo[1, i, 0], echo[1, i, 1], echo[1, i, 2] = jnp.zeros_like(ex), high[1], high[2]
+        extra[0, 0, 0, i] = low[1] + (y_up(low[0]) - low[0])
+        extra[0, 0, 1, i] = low[2] + (z_up(low[0]) - low[0])
+        extra[0, 1, 0, i] = high[1]
+        extra[0, 1, 1, i] = high[2]
+        return carry
+
+    lax.fori_loop(0, 2 * count, answer, 0, unroll=2)
+    for copy in coefs:
+        copy.wait_recv()
+
+    def answer_again(i, carry):
+        s, p = i // 2, i % 2
+        twin = i + 1 - 2 * p
+        for way in range(2):
+            new = step(
+                s,
+                p,
+                [[echo[way, i, c] for c in range(3)]],
+                lambda c, plane: echo[way, twin, c],
+                lambda k: cland[way],
+                False,
+            )
+            for c in range(3):
+                reply[way, i, c] = new[0][c]
+        return carry
+
+    lax.fori_loop(0, 2 * count, answer_again, 0, unroll=2)
+
+    weight_low, weight_high = RELAX * has_before, RELAX * has_after
+    for copy in flows[0]:
+        copy.wait_recv()
     meet(2)
 
-    def products(s, carry):
+    def arrival_0(i, carry):
+        got = [[land[0, way, j, i].astype(jnp.float32) for j in range(2)] for way in range(2)]
+        low = inflow_low(got[0][0], got[0][1], weight_low)
+        high = inflow_high(got[1][0], got[1][1], weight_high)
+        zero = jnp.zeros((height, breadth), jnp.float32)
+        for c in range(3):
+            delta_1[i, c, 0] = low[c] + zero
+            delta_1[i, c, last] = high[c]
+            for plane in range(1, last):
+                delta_1[i, c, plane] = zero
+        near = [alone_1[i, c, 0] + low[c] for c in range(3)]
+        ex, ey, ez = [alone_1[i, c, last] + high[c] for c in range(3)]
+        low = inflow_high(near[1], near[2], RELAX)
+        low = [reply[0, i, c] + low[c] for c in range(3)]
+        high = inflow_low(ey + (y_up(ex) - ex), ez + (z_up(ex) - ex), RELAX)
+        extra[1, 0, 0, i] = low[1] + (y_up(low[0]) - low[0])
+        extra[1, 0, 1, i] = low[2] + (z_up(low[0]) - low[0])
+        extra[1, 1, 0, i] = reply[1, i, 1] + high[1]
+        extra[1, 1, 1, i] = reply[1, i, 2] + high[2]
+        return carry
+
+    lax.fori_loop(0, 2 * count, arrival_0, 0, unroll=2)
+    sweep(held(delta_1), delta_2, False)
+
+    def total_inflow(k, i):
+        got = [
+            [land[k, way, j, i].astype(jnp.float32) + extra[k - 1, way, j, i] for j in range(2)]
+            for way in range(2)
+        ]
+        low = inflow_low(got[0][0], got[0][1], weight_low)
+        return low, inflow_high(got[1][0], got[1][1], weight_high)
+
+    for copy in flows[1]:
+        copy.wait_recv()
+
+    def arrival_1(i, carry):
+        low, high = total_inflow(1, i)
+        for c in range(3):
+            if c > 0:
+                delta_2[i, c, 0] = delta_2[i, c, 0] + low[c]
+            delta_2[i, c, last] = delta_2[i, c, last] + high[c]
+        return carry
+
+    lax.fori_loop(0, 2 * count, arrival_1, 0, unroll=2)
+    sweep(held(delta_2), delta_3, False)
+
+    slots = [0, last] + list(range(1, last))
+
+    def product(s, plane, real_part, imag_part):
         g = group[s]
         angular = angular_of(s)
-        for plane in range(depth):
-            real = jnp.zeros((height, breadth), jnp.float32)
-            imag = jnp.zeros((height, breadth), jnp.float32)
-            for c in range(3):
-                fr, fi = back[g, 0, c, plane], back[g, 1, c, plane]
-                ar, ai = third[2 * s, c, depth + plane], third[2 * s + 1, c, depth + plane]
-                real += fr * ar - fi * ai
-                imag += fr * ai + fi * ar
-            coef = angular * cond[plane]
-            rows[rx, plane, 2 * s] = (coef * real).astype(jnp.bfloat16)
-            rows[rx, plane, 2 * s + 1] = (coef * imag).astype(jnp.bfloat16)
-        return carry
-
-    lax.fori_loop(0, count, products, 0)
-
-    edges = [
-        pltpu.make_async_remote_copy(
-            rows.at[rx, pl.ds(start, 2)],
-            rland.at[way],
-            rsend_sem.at[way],
-            rrecv_sem.at[way],
-            device_id=target,
+        real = jnp.zeros((height, breadth), jnp.float32)
+        imag = jnp.zeros((height, breadth), jnp.float32)
+        for c in range(3):
+            fr, fi = back[g, 0, c, plane], back[g, 1, c, plane]
+            real += fr * real_part[c] - fi * imag_part[c]
+            imag += fr * imag_part[c] + fi * real_part[c]
+        coef = angular * cond[plane]
+        rows[rx, slots.index(plane), 2 * s] = (coef * real).astype(jnp.bfloat16)
+        rows[rx, slots.index(plane), 2 * s + 1] = (coef * imag).astype(jnp.bfloat16)
+
+    def swept(i, plane):
+        return [alone_3[i, c, plane] + delta_3[i, c, plane] for c in range(3)]
+
+    def inner_products(s, carry):
+        for plane in range(1, last):
+            product(s, plane, swept(2 * s, plane), swept(2 * s + 1, plane))
+        return carry
+
+    lax.fori_loop(0, count, inner_products, 0, unroll=2)
+
+    def edge(part, way):
+        plane = ((last - 1, 1), (last, 0))[part][way]
+        place = ((0, 1), (1, 0))[part][way]
+        return pltpu.make_async_remote_copy(
+            rows.at[rx, slots.index(plane)],
+            rland.at[way, place],
+            rsend_sem.at[part, way],
+            rrecv_sem.at[part, way],
+            device_id=(after, before)[way],
             device_id_type=MESH,
         )
-        for way, target, start in ((0, after, depth - 2), (1, before, 0))
-    ]
-    gather = [
-        pltpu.make_async_remote_copy(
-            rows.at[rx],
-            rows.at[rx],
-            gsend_sem.at[k],
-            grecv_sem.at[k],
-            device_id=target,
+
+    def to_group(part, k):
+        span = (pl.ds(2, depth - 2), pl.ds(0, 2))[part]
+        return pltpu.make_async_remote_copy(
+            rows.at[rx, span],
+            rows.at[rx, span],
+            gsend_sem.at[part, k],
+            grecv_sem.at[part, k],
+            device_id=others[k],
             device_id_type=MESH,
         )
-        for k, target in enumerate(others)
-    ]
-    for copy in gather + edges:
+
+    edges = [edge(part, way) for part in range(2) for way in range(2)]
+    gather = [to_group(part, k) for part in range(2) for k in range(rx_peers - 1)]
+    for copy in gather[: rx_peers - 1] + edges[:2]:
+        copy.start()
+    for copy in flows[2]:
+        copy.wait_recv()
+
+    def outer_products(s, carry):
+        parts = []
+        for i in (2 * s, 2 * s + 1):
+            low, high = total_inflow(2, i)
+            near, far = swept(i, 0), swept(i, last)
+            parts.append(
+                ([near[c] + low[c] for c in range(3)], [far[c] + high[c] for c in range(3)])
+            )
+        product(s, 0, parts[0][0], parts[1][0])
+        product(s, last, parts[0][1], parts[1][1])
+        return carry
+
+    lax.fori_loop(0, count, outer_products, 0, unroll=2)
+    for copy in gather[rx_peers - 1 :] + edges[2:]:
         copy.start()
     meet(len(meetings))
     for copy in edges:
@@ -350,7 +457,7 @@
     def smoothing(r, carry):
         planes = (
             [rland[0, k, r].astype(jnp.float32) * has_before for k in range(2)]
-            + [rows[rx, k, r].astype(jnp.float32) for k in range(depth)]
+            + [rows[rx, slots.index(k), r].astype(jnp.float32) for k in range(depth)]
             + [rland[1, k, r].astype(jnp.float32) * has_after for k in range(2)]
         )
         for step in range(2):
@@ -376,35 +483,38 @@
             smooth[r, k] = planes[k].astype(jnp.bfloat16)
         return carry
 
-    lax.fori_loop(0, 2 * count, smoothing, 0)
+    lax.fori_loop(0, 2 * count, smoothing, 0, unroll=2)
 
     for copy in gather:
         copy.wait_recv()
+
+    wide = 2 * count * rx_peers
 
     def dots(b, carry):
         peer, r = b // (2 * count), b % (2 * count)
         for a in range(2 * count):
             total = jnp.zeros((8, breadth), jnp.float32)
             for k in range(depth):
-                product = smooth[a, k].astype(jnp.float32) * rows[peer, k, r].astype(jnp.float32)
+                left = smooth[a, k].astype(jnp.float32)
+                product = left * rows[peer, slots.index(k), r].astype(jnp.float32)
                 for j in range(height // 8):
                     total += product[8 * j : 8 * j + 8]
             sums[a, b] = jnp.sum(total, axis=0)
         return carry
 
-    lax.fori_loop(0, 2 * count * rx_peers, dots, 0)
-    ones = jnp.ones((8, breadth), jnp.float32)
-    wide = 2 * count * rx_peers
+    lax.fori_loop(0, wide, dots, 0)
+    ones = jnp.ones((8, breadth), jnp.bfloat16)
+    by_lane = sums[...].reshape(2 * count * wide, breadth)
+    high = by_lane.astype(jnp.bfloat16)
+    low = (by_lane - high.astype(jnp.float32)).astype(jnp.bfloat16)
+    lanes = [
+        lax.dot_general(
+            ones, part, (((1,), (1,)), ((), ())), preferred_element_type=jnp.float32
+        )
+        for part in (high, low)
+    ]
     line_sums[column] = jnp.zeros(line_sums.shape[1:], jnp.float32)
-    for a in range(2 * count):
-        lanes = lax.dot_general(
-            ones,
-            sums[a],
-            (((1,), (1,)), ((), ())),
-            precision=lax.Precision.HIGHEST,
-            preferred_element_type=jnp.float32,
-        )
-        line_sums[column, a : a + 1, 0:wide] = lanes[0:1]
+    line_sums[column, :, 0 : 2 * count * wide] = (lanes[0] + lanes[1])[0:1]
 
     step_one = [
         pltpu.make_async_remote_copy(
@@ -440,8 +550,9 @@
         copy.wait_recv()
     total = jnp.sum(plane_sums[...], axis=0)
     cells = depth * height * breadth * peers
-    block_ref[...] = total[0 : 2 * count, 0:wide] / cells
-    for copy in sum(stages, []) + edges + gather + step_one + step_two:
+    for a in range(2 * count):
+        block_ref[a : a + 1, :] = total[:, a * wide : (a + 1) * wide] / cells
+    for copy in sum(flows, []) + coefs + edges + gather + step_one + step_two:
         copy.wait_send()
 
 
@@ -486,26 +597,26 @@
             pltpu.SMEM(recv_cell.shape, jnp.int32),
             pltpu.SMEM(src_group.shape, jnp.int32),
             pltpu.SMEM(group_freq.shape, jnp.int32),
-            vmem((depth, 3, rows) + plane, b16),
-            vmem((2, rows) + plane, b16),
-            vmem((depth,) + plane, b16),
-            vmem((2, depth, 3, rows) + plane, b16),
-            vmem((2, depth) + plane, b16),
-            vmem((rows, 3, 3 * depth) + plane, f32),
-            vmem((rows, 3, 3 * depth) + plane, f32),
-            vmem((rows, 3, 3 * depth) + plane, f32),
+            vmem((ITERS, 2, 2, rows) + plane, b16),
+            vmem((ITERS, 2, 2, rows) + plane, b16),
+            vmem((2,) + plane, f32),
+        ]
+        + [vmem((rows, 3, depth) + plane, f32)] * 6
+        + [vmem((2, rows, 3) + plane, f32)] * 2
+        + [
+            vmem((ITERS - 1, 2, 2, rows) + plane, f32),
             vmem((rx_peers, depth, rows) + plane, b16),
             vmem((2, 2, rows) + plane, b16),
             vmem((rows, wide, breadth), f32),
-            vmem((columns, 8, 128), f32),
-            vmem((lines, 8, 128), f32),
+            vmem((columns, 1, breadth), f32),
+            vmem((lines, 1, breadth), f32),
             dma((7,)),
-            dma((2, depth + 1)),
-            dma((2, depth + 1)),
-            dma((2,)),
-            dma((2,)),
-            dma((rx_peers - 1,)),
-            dma((rx_peers - 1,)),
+            dma((2, ITERS + 1)),
+            dma((2, ITERS + 1)),
+            dma((2, 2)),
+            dma((2, 2)),
+            dma((2, rx_peers - 1)),
+            dma((2, rx_peers - 1)),
             dma((2, max(lines, columns) - 1)),
             dma((2, max(lines, columns) - 1)),
             pltpu.SemaphoreType.REGULAR((4,)),

time: 52.4 us -> 46.2 us (0.88)
  the two profiles are of different devices: /device:TPU:4 before, /device:TPU:1 now
where the time goes in v3:
time: 46.2 us; the launch traced here: 46 us
  Pallas kernels  44.2 us (96%)
  local copies, waits for them, and re-layouts  1.22 us (3%)
  between operations  0.64 us (1%)
    pallas_call x1, Pallas kernels, shards(): pl.pallas_call(functools.partial(kernel, peers, lines, rx_peers), name='i...  44.2 us
    unnamed x2, local copies, waits for them, and re-layouts  1.22 us

profile of v3, /device:TPU:1, one launch (start us, length us, event | category | flops | bytes accessed | tf_op | source)
XLA Modules:
  0.0 46.0 jit_solution(15438550317705982870)
XLA Ops:
  0.6 44.2 %inversion_step.1 = (f32[4,16]{1,0:T(4,128)S(1)}, bf16[4,3,32,128]{3,2,1,0:T(8,128)(2,1)S(1)}) custom-call(f32[3,32,128]{2,1,0:T(8,128)} %cond_hbm.1, f32[4,2,3,3,32,128]{5,4,3,2,1,0:T(8,128)} %back_hbm.1, f32[2,2,3,3,32,128]{5,4,3,2,1,0:T(8,128)} %warm_hbm.1, f32[2,2,3]{2,1,0:T(2,128)} %weight_hbm.1, s32[2]{0:T(128)} %cell_hbm.1, s32[2]{0:T(128)} %group_hbm.1, ...), custom_call_target="tpu_custom_call" | custom-call | tf_op jit(solution)/shard_map/inversion_step/pallas_call | solution.py:583
  44.8 0.6 %copy.11 = f32[4,16]{1,0:T(4,128)} copy(f32[4,16]{1,0:T(4,128)S(1)} %get-tuple-element.6) | data formatting | bytes 512
  45.4 0.6 %copy.12 = bf16[2,2,3,32,128]{4,3,2,1,0:T(8,128)(2,1)} copy(bf16[2,2,3,32,128]{4,3,2,1,0:T(8,128)(2,1)S(1)} %bitcast.1) | data formatting | bytes 196608

commit v4 on v3

--- a/solution.py
+++ b/solution.py
@@ -47,6 +47,7 @@
     extra,
     rows,
     rland,
+    twice,
     sums,
     line_sums,
     plane_sums,
@@ -71,7 +72,10 @@
     column = me % columns
     after = (rx, (me + 1) % peers)
     before = (rx, (me + peers - 1) % peers)
-    others = [((rx + k) % rx_peers, me) for k in range(1, rx_peers)]
+    others = []
+    for k in range(0, rx_peers, 2):
+        place = (rx + k) % rx_peers
+        others += [(place, me)] * (k > 0) + [(place + 1 - 2 * (place % 2), me)]
 
     def at(line, column):
         return (rx, (line % lines) * columns + column % columns)
@@ -80,50 +84,54 @@
     across = [at(line + k, column) for k in range(1, lines)]
     rows_y = lines // 2
     half = (line // rows_y) * rows_y
+    high_x = max(rx_peers // 2, 1)
 
     def beside(k):
         return at(half + (line + k + rows_y) % rows_y, column)
 
+    def along_x(k):
+        place = (2 * (rx // 2) + line // rows_y + k + 2 * high_x) % (2 * high_x)
+        place_line = (place % 2) * rows_y + line % rows_y
+        return (2 * (place // 2) + rx % 2, place_line * columns + column)
+
     opposite = at(line + rows_y, column)
-
+    core = others[0]
+
+    starts = [(s, p) for s in range(count) for p in range(2)]
     loads = [
         pltpu.make_async_copy(src, dst, load_sem.at[i])
         for i, (src, dst) in enumerate(
-            (
-                (warm_hbm, warm),
+            [(warm_hbm.at[s, p], warm.at[s, p]) for s, p in starts]
+            + [
                 (cond_hbm, cond),
                 (weight_hbm, weight),
                 (cell_hbm, cell),
                 (group_hbm, group),
                 (freq_hbm, freq),
                 (back_hbm, back),
-            )
+            ]
         )
     ]
-    for load in loads:
-        load.start()
     barrier = pltpu.get_barrier_semaphore()
-    near = [at(line, column + 1), at(line, column - 1), opposite]
-    if rows_y > 1:
-        near += [beside(1), beside(-1)]
-    partners = [before, after] + near + others
+    ring_z = [at(line, column + 1), at(line, column - 1)]
+    ring_x = [along_x(1), along_x(-1)]
+    ring_y = [beside(1), beside(-1)] if rows_y > 1 else []
+    partners = [before, after, core] + ring_z + ring_x + ring_y
     for partner in partners:
         pl.semaphore_signal(barrier, inc=1, device_id=partner, device_id_type=MESH)
-
-    meetings = []
-    reach, y_steps = 1, 0
+    for load in loads[:-1]:
+        load.start()
+
+    meetings = [list(ring_x), [core], [opposite]]
+    reach, k = 1, 0
     while reach < max(columns, rows_y) // 2:
-        targets = []
+        if k == len(meetings):
+            meetings.append([])
         if reach < columns // 2:
-            targets += [at(line, column + reach), at(line, column - reach)]
+            meetings[k] += [at(line, column + reach), at(line, column - reach)]
         if reach < rows_y // 2:
-            targets += [beside(reach), beside(-reach)]
-            y_steps += 1
-        meetings.append(targets)
-        reach *= 2
-    if len(meetings) == y_steps:
-        meetings.append([])
-    meetings[y_steps].append(opposite)
+            meetings[k] += [beside(reach), beside(-reach)]
+        reach, k = 2 * reach, k + 1
     taken = []
 
     def meet(steps):
@@ -138,7 +146,7 @@
                     )
             taken.append(step)
 
-    for load in loads[:2]:
+    for load in loads[: len(starts) + 1]:
         load.wait()
     iy = lax.broadcasted_iota(jnp.int32, (height, breadth), 0)
     iz = lax.broadcasted_iota(jnp.int32, (height, breadth), 1)
@@ -186,9 +194,10 @@
     coefs = [halo(ITERS, 0, cond.at[last], cland.at[0]), halo(ITERS, 1, cond.at[0], cland.at[1])]
     for copy in flows[0] + coefs:
         copy.start()
+    loads[-1].start()
     meet(1)
 
-    for load in loads[2:]:
+    for load in loads[len(starts) + 1 : -1]:
         load.wait()
     has_before = (me > 0).astype(jnp.float32)
     has_after = (me < peers - 1).astype(jnp.float32)
@@ -308,6 +317,7 @@
         return carry
 
     lax.fori_loop(0, 2 * count, answer, 0, unroll=2)
+    meet(2)
     for copy in coefs:
         copy.wait_recv()
 
@@ -332,7 +342,6 @@
     weight_low, weight_high = RELAX * has_before, RELAX * has_after
     for copy in flows[0]:
         copy.wait_recv()
-    meet(2)
 
     def arrival_0(i, carry):
         got = [[land[0, way, j, i].astype(jnp.float32) for j in range(2)] for way in range(2)]
@@ -403,6 +412,7 @@
             product(s, plane, swept(2 * s, plane), swept(2 * s + 1, plane))
         return carry
 
+    loads[-1].wait()
     lax.fori_loop(0, count, inner_products, 0, unroll=2)
 
     def edge(part, way):
@@ -430,6 +440,7 @@
 
     edges = [edge(part, way) for part in range(2) for way in range(2)]
     gather = [to_group(part, k) for part in range(2) for k in range(rx_peers - 1)]
+    meet(3)
     for copy in gather[: rx_peers - 1] + edges[:2]:
         copy.start()
     for copy in flows[2]:
@@ -450,59 +461,66 @@
     lax.fori_loop(0, count, outer_products, 0, unroll=2)
     for copy in gather[rx_peers - 1 :] + edges[2:]:
         copy.start()
-    meet(len(meetings))
+    def within(f):
+        return f + KAPPA * (y_up(f) + y_down(f) + z_up(f) + z_down(f) - 6.0 * f)
+
+    def smooth_own(r, carry):
+        own = [rows[rx, slots.index(k), r].astype(jnp.float32) for k in range(depth)]
+        once = [within(f) for f in own]
+        for k in range(depth):
+            if k > 0:
+                once[k] += KAPPA * own[k - 1]
+            if k < last:
+                once[k] += KAPPA * own[k + 1]
+        once = [(KAPPA * has_before) * own[0]] + once + [(KAPPA * has_after) * own[last]]
+        for k in range(depth):
+            twice[r, k] = within(once[k + 1]) + KAPPA * (once[k] + once[k + 2])
+        return carry
+
+    lax.fori_loop(0, 2 * count, smooth_own, 0, unroll=2)
     for copy in edges:
         copy.wait_recv()
 
-    def smoothing(r, carry):
-        planes = (
-            [rland[0, k, r].astype(jnp.float32) * has_before for k in range(2)]
-            + [rows[rx, slots.index(k), r].astype(jnp.float32) for k in range(depth)]
-            + [rland[1, k, r].astype(jnp.float32) * has_after for k in range(2)]
-        )
-        for step in range(2):
-            ends = [planes[0], planes[-1]]
-            planes = [
-                planes[k]
-                + KAPPA
-                * (
-                    planes[k - 1]
-                    + planes[k + 1]
-                    + y_up(planes[k])
-                    + y_down(planes[k])
-                    + z_up(planes[k])
-                    + z_down(planes[k])
-                    - 6.0 * planes[k]
-                )
-                for k in range(1, len(planes) - 1)
-            ]
-            if step == 0:
-                planes[0] = planes[0] * has_before
-                planes[-1] = planes[-1] * has_after
+    def smooth_edges(r, carry):
+        value = [twice[r, k] for k in range(depth)]
+        for has, ends, border, inner in (
+            (has_before, (0, 1), 0, 1),
+            (has_after, (1, 0), last, last - 1),
+        ):
+            way = 0 if border == 0 else 1
+            far, near = (rland[way, k, r].astype(jnp.float32) * has for k in ends)
+            value[border] += (2.0 * KAPPA) * within(near) + (KAPPA * KAPPA) * far
+            value[inner] += (KAPPA * KAPPA) * near
         for k in range(depth):
-            smooth[r, k] = planes[k].astype(jnp.bfloat16)
-        return carry
-
-    lax.fori_loop(0, 2 * count, smoothing, 0, unroll=2)
-
-    for copy in gather:
+            rounded = value[k].astype(jnp.bfloat16)
+            smooth[r, k] = rounded
+            twice[r, k] = rounded.astype(jnp.float32)
+        return carry
+
+    lax.fori_loop(0, 2 * count, smooth_edges, 0, unroll=2)
+
+    for copy in gather[:: rx_peers - 1]:
         copy.wait_recv()
 
     wide = 2 * count * rx_peers
 
     def dots(b, carry):
-        peer, r = b // (2 * count), b % (2 * count)
+        peer, r = (rx - rx % 2 + b // (2 * count)) % rx_peers, b % (2 * count)
+        right = [rows[peer, slots.index(k), r].astype(jnp.float32) for k in range(depth)]
         for a in range(2 * count):
             total = jnp.zeros((8, breadth), jnp.float32)
             for k in range(depth):
-                left = smooth[a, k].astype(jnp.float32)
-                product = left * rows[peer, slots.index(k), r].astype(jnp.float32)
+                product = twice[a, k] * right[k]
                 for j in range(height // 8):
                     total += product[8 * j : 8 * j + 8]
-            sums[a, b] = jnp.sum(total, axis=0)
-        return carry
-
-    lax.fori_loop(0, wide, dots, 0)
+            sums[a, peer * (2 * count) + r] = jnp.sum(total, axis=0)
+        return carry
+
+    lax.fori_loop(0, 4 * count, dots, 0, unroll=2)
+    for k in range(1, rx_peers - 1):
+        for copy in gather[k :: rx_peers - 1]:
+            copy.wait_recv()
+    lax.fori_loop(4 * count, wide, dots, 0, unroll=2)
     ones = jnp.ones((8, breadth), jnp.bfloat16)
     by_lane = sums[...].reshape(2 * count * wide, breadth)
     high = by_lane.astype(jnp.bfloat16)
@@ -554,6 +572,17 @@
         block_ref[a : a + 1, :] = total[:, a * wide : (a + 1) * wide] / cells
     for copy in sum(flows, []) + coefs + edges + gather + step_one + step_two:
         copy.wait_send()
+
+
+def deliver(block, smooth, block_out, smooth_out, sem):
+    copies = [
+        pltpu.make_async_copy(smooth, smooth_out, sem.at[0]),
+        pltpu.make_async_copy(block, block_out, sem.at[1]),
+    ]
+    for copy in copies:
+        copy.start()
+    for copy in copies:
+        copy.wait()
 
 
 def shards(conductivity, background, warm_start, data_weight, recv_cell, src_group, group_freq):
@@ -607,10 +636,11 @@
             vmem((ITERS - 1, 2, 2, rows) + plane, f32),
             vmem((rx_peers, depth, rows) + plane, b16),
             vmem((2, 2, rows) + plane, b16),
+            vmem((rows, depth) + plane, f32),
             vmem((rows, wide, breadth), f32),
             vmem((columns, 1, breadth), f32),
             vmem((lines, 1, breadth), f32),
-            dma((7,)),
+            dma((rows + 6,)),
             dma((2, ITERS + 1)),
             dma((2, ITERS + 1)),
             dma((2, 2)),
@@ -619,12 +649,21 @@
             dma((2, rx_peers - 1)),
             dma((2, max(lines, columns) - 1)),
             dma((2, max(lines, columns) - 1)),
-            pltpu.SemaphoreType.REGULAR((4,)),
+            pltpu.SemaphoreType.REGULAR((3,)),
         ],
         compiler_params=pltpu.CompilerParams(
             collective_id=0, has_side_effects=True, vmem_limit_bytes=48 * 2**20
         ),
     )(*pinned)
+    results = [pltpu.with_memory_space_constraint(x, vmem) for x in (block, smoothed)]
+    block, smoothed = pl.pallas_call(
+        deliver,
+        name="deliver",
+        out_shape=(pltpu.HBM((rows, wide), f32), pltpu.HBM((rows, depth) + plane, b16)),
+        in_specs=[pl.BlockSpec(memory_space=vmem)] * 2,
+        out_specs=(hbm, hbm),
+        scratch_shapes=[dma((2,))],
+    )(*results)
     return block, smoothed.reshape((count, 2, depth) + plane)
 
 

time: 46.2 us -> 45.2 us (0.978)
  local copies, waits for them, and re-layouts: 1.22 us -> 0 us
    unnamed x2 -> x0, local copies, waits for them, and re-layouts: 1.22 us -> none
    pallas_call x0 -> x1, Pallas kernels: none -> 0.66 us  [shards(): pl.pallas_call(deliver, name='deliver', out_shape=(pltpu.HBM((rows, wide)...]
    pallas_call x1, Pallas kernels: 44.2 us -> 43.7 us  [shards(): pl.pallas_call(functools.partial(kernel, peers, lines, rx_peers), name='i...]
where the time goes in v4:
time: 45.2 us; the launch traced here: 45 us
  Pallas kernels  44.3 us (98%)
  between operations  0.64 us (1%)
    pallas_call x1, Pallas kernels, shards(): pl.pallas_call(functools.partial(kernel, peers, lines, rx_peers), name='i...  43.7 us

profile of v4, /device:TPU:1, one launch (start us, length us, event | category | flops | bytes accessed | tf_op | source)
XLA Modules:
  0.0 45.0 jit_solution(11870573771231887891)
XLA Ops:
  0.6 43.7 %inversion_step.1 = (f32[4,16]{1,0:T(4,128)S(1)}, bf16[4,3,32,128]{3,2,1,0:T(8,128)(2,1)S(1)}) custom-call(f32[3,32,128]{2,1,0:T(8,128)} %cond_hbm.1, f32[4,2,3,3,32,128]{5,4,3,2,1,0:T(8,128)} %back_hbm.1, f32[2,2,3,3,32,128]{5,4,3,2,1,0:T(8,128)} %warm_hbm.1, f32[2,2,3]{2,1,0:T(2,128)} %weight_hbm.1, s32[2]{0:T(128)} %cell_hbm.1, s32[2]{0:T(128)} %group_hbm.1, ...), custom_call_target="tpu_custom_call" | custom-call | tf_op jit(solution)/shard_map/inversion_step/pallas_call | solution.py:612
  44.3 0.7 %deliver.1 = (f32[4,16]{1,0:T(4,128)}, bf16[4,3,32,128]{3,2,1,0:T(8,128)(2,1)}) custom-call(f32[4,16]{1,0:T(4,128)S(1)} %get-tuple-element.6.block, bf16[4,3,32,128]{3,2,1,0:T(8,128)(2,1)S(1)} %get-tuple-element.7.smooth), custom_call_target="tpu_custom_call" | custom-call | tf_op jit(solution)/shard_map/deliver/pallas_call | solution.py:659

commit v5 on v4

--- a/solution.py
+++ b/solution.py
@@ -112,6 +112,8 @@
             ]
         )
     ]
+    for load in loads[: len(starts) + 1]:
+        load.start()
     barrier = pltpu.get_barrier_semaphore()
     ring_z = [at(line, column + 1), at(line, column - 1)]
     ring_x = [along_x(1), along_x(-1)]
@@ -119,7 +121,7 @@
     partners = [before, after, core] + ring_z + ring_x + ring_y
     for partner in partners:
         pl.semaphore_signal(barrier, inc=1, device_id=partner, device_id_type=MESH)
-    for load in loads[:-1]:
+    for load in loads[len(starts) + 1 : -1]:
         load.start()
 
     meetings = [list(ring_x), [core], [opposite]]
@@ -429,19 +431,20 @@
 
     def to_group(part, k):
         span = (pl.ds(2, depth - 2), pl.ds(0, 2))[part]
+        slot = (rx, rx, (rx + 2) % rx_peers)[k]
         return pltpu.make_async_remote_copy(
-            rows.at[rx, span],
-            rows.at[rx, span],
+            rows.at[slot, span],
+            rows.at[slot, span],
             gsend_sem.at[part, k],
             grecv_sem.at[part, k],
-            device_id=others[k],
+            device_id=others[(0, 1, 0)[k]],
             device_id_type=MESH,
         )
 
     edges = [edge(part, way) for part in range(2) for way in range(2)]
-    gather = [to_group(part, k) for part in range(2) for k in range(rx_peers - 1)]
+    gather = [[to_group(part, k) for k in range(rx_peers - 1)] for part in range(2)]
     meet(3)
-    for copy in gather[: rx_peers - 1] + edges[:2]:
+    for copy in gather[0][:2] + edges[:2]:
         copy.start()
     for copy in flows[2]:
         copy.wait_recv()
@@ -459,7 +462,7 @@
         return carry
 
     lax.fori_loop(0, count, outer_products, 0, unroll=2)
-    for copy in gather[rx_peers - 1 :] + edges[2:]:
+    for copy in gather[1][:2] + edges[2:]:
         copy.start()
     def within(f):
         return f + KAPPA * (y_up(f) + y_down(f) + z_up(f) + z_down(f) - 6.0 * f)
@@ -478,6 +481,10 @@
         return carry
 
     lax.fori_loop(0, 2 * count, smooth_own, 0, unroll=2)
+    if rx_peers > 2:
+        for part in range(2):
+            gather[part][1].wait_recv()
+            gather[part][2].start()
     for copy in edges:
         copy.wait_recv()
 
@@ -499,9 +506,8 @@
 
     lax.fori_loop(0, 2 * count, smooth_edges, 0, unroll=2)
 
-    for copy in gather[:: rx_peers - 1]:
-        copy.wait_recv()
-
+    for part in range(2):
+        gather[part][0].wait_recv()
     wide = 2 * count * rx_peers
 
     def dots(b, carry):
@@ -517,9 +523,9 @@
         return carry
 
     lax.fori_loop(0, 4 * count, dots, 0, unroll=2)
-    for k in range(1, rx_peers - 1):
-        for copy in gather[k :: rx_peers - 1]:
-            copy.wait_recv()
+    if rx_peers > 2:
+        for part in range(2):
+            gather[part][2].wait_recv()
     lax.fori_loop(4 * count, wide, dots, 0, unroll=2)
     ones = jnp.ones((8, breadth), jnp.bfloat16)
     by_lane = sums[...].reshape(2 * count * wide, breadth)
@@ -570,7 +576,7 @@
     cells = depth * height * breadth * peers
     for a in range(2 * count):
         block_ref[a : a + 1, :] = total[:, a * wide : (a + 1) * wide] / cells
-    for copy in sum(flows, []) + coefs + edges + gather + step_one + step_two:
+    for copy in sum(flows, []) + coefs + edges + gather[0] + gather[1] + step_one + step_two:
         copy.wait_send()
 
 

time: 45.2 us -> 45 us (level)
  no operation moved by 1% of the time
where the time goes in v5:
time: 45 us; the launch traced here: 44.9 us
  Pallas kernels  44.2 us (98%)
  between operations  0.64 us (1%)
    pallas_call x1, Pallas kernels, shards(): pl.pallas_call(functools.partial(kernel, peers, lines, rx_peers), name='i...  43.6 us

profile of v5, /device:TPU:1, one launch (start us, length us, event | category | flops | bytes accessed | tf_op | source)
XLA Modules:
  0.0 44.9 jit_solution(225422755165079808)
XLA Ops:
  0.6 43.6 %inversion_step.1 = (f32[4,16]{1,0:T(4,128)S(1)}, bf16[4,3,32,128]{3,2,1,0:T(8,128)(2,1)S(1)}) custom-call(f32[3,32,128]{2,1,0:T(8,128)} %cond_hbm.1, f32[4,2,3,3,32,128]{5,4,3,2,1,0:T(8,128)} %back_hbm.1, f32[2,2,3,3,32,128]{5,4,3,2,1,0:T(8,128)} %warm_hbm.1, f32[2,2,3]{2,1,0:T(2,128)} %weight_hbm.1, s32[2]{0:T(128)} %cell_hbm.1, s32[2]{0:T(128)} %group_hbm.1, ...), custom_call_target="tpu_custom_call" | custom-call | tf_op jit(solution)/shard_map/inversion_step/pallas_call | solution.py:618
  44.2 0.7 %deliver.1 = (f32[4,16]{1,0:T(4,128)}, bf16[4,3,32,128]{3,2,1,0:T(8,128)(2,1)}) custom-call(f32[4,16]{1,0:T(4,128)S(1)} %get-tuple-element.6.block, bf16[4,3,32,128]{3,2,1,0:T(8,128)(2,1)S(1)} %get-tuple-element.7.smooth), custom_call_target="tpu_custom_call" | custom-call | tf_op jit(solution)/shard_map/deliver/pallas_call | solution.py:665
